TPU v7x, 128 devices: a whole 4x4x4 slice. The times are simulated.
128 devices in a mesh: ctx: 8 (over z, y_hi), shard: 16 (over x, y_lo, core).
Axes of the slice: x: 4, y: 4 (y_hi: 2, y_lo: 2; y = y_hi * 2 + y_lo), z: 4, core: 2. Of those that a mesh axis runs over, the one named last changes fastest.
Arguments:
- inputs: bfloat16 [16, 2048, 1024], P('shard', 'ctx'), may hold values from -6 to 6
- cotangent: bfloat16 [16, 2048, 1024], P('shard', 'ctx'), may hold values from -6 to 6
- w_qkv: bfloat16 [1024, 3072], P('shard'), may hold values from -0.1875 to 0.1875
- bias_query: bfloat16 [1024], P('shard'), may hold values from -4 to 4
- bias_value: bfloat16 [1024], P('shard'), may hold values from -0.3125 to 0.3125
- w_out: bfloat16 [1024, 1024], P('shard'), may hold values from -4 to 4
- bias_out: bfloat16 [1024], P('shard'), may hold values from -4 to 4
- gain_attn: bfloat16 [1024], P('shard'), may hold values from 0.099609375 to 1.8984375
- shift_attn: bfloat16 [1024], P('shard'), may hold values from -4 to 4
- w_up: bfloat16 [1024, 4096], P('shard'), may hold values from -0.1875 to 0.1875
- bias_up: bfloat16 [4096], P('shard'), may hold values from -4 to 4
- w_down: bfloat16 [4096, 1024], P('shard'), may hold values from -0.09375 to 0.09375
- bias_down: bfloat16 [1024], P('shard'), may hold values from -4 to 4
- gain_ffn: bfloat16 [1024], P('shard'), may hold values from 0.099609375 to 1.8984375
- shift_ffn: bfloat16 [1024], P('shard'), may hold values from -4 to 4
Outputs:
- outputs: bfloat16 [16, 2048, 1024], P('shard', 'ctx')
- input_grad: float32 [16, 2048, 1024], P('shard', 'ctx')
- grad_w_qkv: float32 [1024, 3072], P('shard')
- grad_bias_query: float32 [1024], P('shard')
- grad_bias_value: float32 [1024], P('shard')
- grad_w_out: float32 [1024, 1024], P('shard')
- grad_bias_out: float32 [1024], P('shard')
- grad_gain_attn: float32 [1024], P('shard')
- grad_shift_attn: float32 [1024], P('shard')
- grad_w_up: float32 [1024, 4096], P('shard')
- grad_bias_up: float32 [4096], P('shard')
- grad_w_down: float32 [4096, 1024], P('shard')
- grad_bias_down: float32 [1024], P('shard')
- grad_gain_ffn: float32 [1024], P('shard')
- grad_shift_ffn: float32 [1024], P('shard')
All inputs are finite; a program needn't handle non-finite values.
Results may differ from a plain program's by a relative error of at most 0.025.
Values may be sent and summed in bfloat16 or wider, within the bound.
No kernel may reach another device: no remote copies, remote signals or barrier semaphores. Data moves between devices by JAX's collectives and lax.ppermute only.
A program may use at most 128 MiB of HBM per device.

v0:
```python
from functools import partial
import math

import jax
import jax.numpy as jnp
from jax import lax
from jax.sharding import PartitionSpec as P

D = 1024
HEADS = 16
HD = 64


ln_epsilon = 1e-12


def layer_norm(hidden, norm_gain, norm_shift):
    centered = hidden - jnp.mean(hidden, axis=-1, keepdims=True)
    deviation = lax.rsqrt(jnp.mean(centered * centered, axis=-1, keepdims=True) + ln_epsilon)
    normal = centered * deviation
    return (normal * norm_gain + norm_shift, normal, deviation)


def norm_back(upstream, normal, deviation, norm_gain):
    scaled = upstream * norm_gain
    centred = (
        scaled
        - jnp.mean(scaled, axis=-1, keepdims=True)
        - normal * jnp.mean(scaled * normal, axis=-1, keepdims=True)
    )
    return (deviation * centred, jnp.sum(upstream * normal, 0), jnp.sum(upstream, 0))


def key_blocks(gathered):
    piece_rows = gathered[0].shape[0]
    block_rows = math.gcd(piece_rows, 512)
    blocks = tuple(
        (
            member.reshape((piece_rows // block_rows, block_rows) + member.shape[1:])
            for member in gathered
        )
    )
    return (blocks, block_rows)


def shards(
    inputs,
    cotangent,
    w_qkv,
    bias_query,
    bias_value,
    w_out,
    bias_out,
    gain_attn,
    shift_attn,
    w_up,
    bias_up,
    w_down,
    bias_down,
    gain_ffn,
    shift_ffn,
):
    tokens = inputs[0]
    block_len = tokens.shape[0]
    score_scale = HD ** (-0.5)
    gathered = (
        lax.all_gather(w_qkv, "shard", axis=0, tiled=True),
        lax.all_gather(bias_query, "shard", axis=0, tiled=True),
        lax.all_gather(bias_value, "shard", axis=0, tiled=True),
        lax.all_gather(w_out, "shard", axis=0, tiled=True),
        lax.all_gather(bias_out, "shard", axis=0, tiled=True),
        lax.all_gather(gain_attn, "shard", axis=0, tiled=True),
        lax.all_gather(shift_attn, "shard", axis=0, tiled=True),
        lax.all_gather(w_up, "shard", axis=0, tiled=True),
        lax.all_gather(bias_up, "shard", axis=0, tiled=True),
        lax.all_gather(w_down, "shard", axis=0, tiled=True),
        lax.all_gather(bias_down, "shard", axis=0, tiled=True),
        lax.all_gather(gain_ffn, "shard", axis=0, tiled=True),
        lax.all_gather(shift_ffn, "shard", axis=0, tiled=True),
    )
    (
        full_qkv,
        full_bias_query,
        full_bias_value,
        full_out,
        full_bias_out,
        full_gain_attn,
        full_shift_attn,
        full_up,
        full_bias_up,
        full_down,
        full_bias_down,
        full_gain_ffn,
        full_shift_ffn,
    ) = gathered
    bias_all = jnp.concatenate(
        [full_bias_query, jnp.zeros_like(full_bias_query), full_bias_value]
    ).astype(jnp.float32)
    qkv_low = (jnp.dot(tokens, full_qkv, preferred_element_type=jnp.float32) + bias_all).astype(
        jnp.bfloat16
    )
    queries = qkv_low[:, :D].reshape(block_len, HEADS, HD)
    keys = qkv_low[:, D : 2 * D].reshape(block_len, HEADS, HD)
    values = qkv_low[:, 2 * D :].reshape(block_len, HEADS, HD)
    start_state = (
        jnp.full((block_len, HEADS), -jnp.inf, jnp.float32),
        jnp.zeros((block_len, HEADS), jnp.float32),
        jnp.zeros((block_len, HEADS, HD), jnp.float32),
    )
    blocks, block_rows = key_blocks(
        (
            lax.all_gather(keys, "ctx", axis=0, tiled=True),
            lax.all_gather(values, "ctx", axis=0, tiled=True),
        )
    )

    def absorb_advance(state, key_block):
        peak_value, row_total, weighted = state
        block_keys, block_values = key_block
        scores = (
            jnp.einsum("qhe,khe->qhk", queries, block_keys, preferred_element_type=jnp.float32)
            * score_scale
        )
        new_peak = jnp.maximum(peak_value, jnp.max(scores, axis=-1))
        rescale = jnp.exp(peak_value - new_peak)
        expo = jnp.exp(scores - new_peak[..., None])
        row_total = row_total * rescale + jnp.sum(expo, axis=-1)
        weighted = weighted * rescale[..., None] + jnp.einsum(
            "qhk,khe->qhe",
            expo.astype(jnp.bfloat16),
            block_values,
            preferred_element_type=jnp.float32,
        )
        return ((new_peak, row_total, weighted), None)

    state, unused = lax.scan(absorb_advance, start_state, blocks)
    peak_value, row_total, weighted = state
    log_total = peak_value + jnp.log(row_total)
    attended = weighted / row_total[..., None]
    attended_low = attended.reshape(block_len, D).astype(jnp.bfloat16)
    attn = jnp.dot(
        attended_low, full_out, preferred_element_type=jnp.float32
    ) + full_bias_out.astype(jnp.float32)
    first, normal_attn, deviation_attn = layer_norm(
        tokens.astype(jnp.float32) + attn,
        full_gain_attn.astype(jnp.float32),
        full_shift_attn.astype(jnp.float32),
    )
    first_low = first.astype(jnp.bfloat16)
    pre = jnp.dot(first_low, full_up, preferred_element_type=jnp.float32) + full_bias_up.astype(
        jnp.float32
    )
    activated, gelu_pull = jax.vjp(partial(jax.nn.gelu, approximate=False), pre)
    activated_low = activated.astype(jnp.bfloat16)
    ffn = jnp.dot(
        activated_low, full_down, preferred_element_type=jnp.float32
    ) + full_bias_down.astype(jnp.float32)
    outputs, normal_ffn, deviation_ffn = layer_norm(
        first + ffn, full_gain_ffn.astype(jnp.float32), full_shift_ffn.astype(jnp.float32)
    )
    back_qkv, back_out, back_up, back_down, back_gain_attn, back_gain_ffn = (
        lax.all_gather(w_qkv, "shard", axis=0, tiled=True),
        lax.all_gather(w_out, "shard", axis=0, tiled=True),
        lax.all_gather(w_up, "shard", axis=0, tiled=True),
        lax.all_gather(w_down, "shard", axis=0, tiled=True),
        lax.all_gather(gain_attn, "shard", axis=0, tiled=True),
        lax.all_gather(gain_ffn, "shard", axis=0, tiled=True),
    )
    upstream = cotangent[0].astype(jnp.float32)
    dffn, grad_gain_ffn, grad_shift_ffn = norm_back(
        upstream, normal_ffn, deviation_ffn, back_gain_ffn.astype(jnp.float32)
    )
    dffn_low = dffn.astype(jnp.bfloat16)
    grad_bias_down = jnp.sum(dffn_low.astype(jnp.float32), 0)
    grad_w_down = lax.psum_scatter(
        jnp.einsum(
            "tf,td->fd",
            lax.slice_in_dim(activated_low, 0, lax.axis_size("shard") * w_down.shape[0], axis=1),
            dffn_low,
            preferred_element_type=jnp.float32,
        ).astype(jnp.bfloat16),
        "shard",
        scatter_dimension=0,
        tiled=True,
    )
    dpre = gelu_pull(
        jnp.einsum("td,fd->tf", dffn_low, back_down, preferred_element_type=jnp.float32)
    )[0]
    dpre_low = dpre.astype(jnp.bfloat16)
    grad_bias_up = jnp.sum(dpre_low.astype(jnp.float32), 0)
    grad_w_up = lax.psum_scatter(
        jnp.einsum("td,tf->df", first_low, dpre_low, preferred_element_type=jnp.float32).astype(
            jnp.bfloat16
        ),
        "shard",
        scatter_dimension=0,
        tiled=True,
    )
    dfirst = dffn + jnp.einsum("tf,df->td", dpre_low, back_up, preferred_element_type=jnp.float32)
    dmixed, grad_gain_attn, grad_shift_attn = norm_back(
        dfirst, normal_attn, deviation_attn, back_gain_attn.astype(jnp.float32)
    )
    dattn_low = dmixed.astype(jnp.bfloat16)
    grad_bias_out = jnp.sum(dattn_low.astype(jnp.float32), 0)
    grad_w_out = lax.psum_scatter(
        jnp.einsum("td,te->de", attended_low, dattn_low, preferred_element_type=jnp.float32).astype(
            jnp.bfloat16
        ),
        "shard",
        scatter_dimension=0,
        tiled=True,
    )
    dattended = (
        jnp.einsum("td,ed->te", dattn_low, back_out, preferred_element_type=jnp.float32)
        .astype(jnp.bfloat16)
        .reshape(block_len, HEADS, HD)
    )
    delta = jnp.sum(dattended.astype(jnp.float32) * attended, axis=-1)
    total_len = block_len * lax.axis_size("ctx")
    grad_start = (
        jnp.zeros((block_len, HEADS, HD), jnp.float32),
        jnp.zeros((total_len, HEADS, HD), jnp.float32),
        jnp.zeros((total_len, HEADS, HD), jnp.float32),
    )
    blocks, block_rows = key_blocks(
        (
            lax.all_gather(keys, "ctx", axis=0, tiled=True),
            lax.all_gather(values, "ctx", axis=0, tiled=True),
        )
    )

    def reflect_advance(state, indexed):
        grad_query, key_total, value_total = state
        block_index, key_block = indexed
        block_keys, block_values = key_block
        scores = (
            jnp.einsum("qhe,khe->qhk", queries, block_keys, preferred_element_type=jnp.float32)
            * score_scale
        )
        attention = jnp.exp(scores - log_total[..., None])
        dprobs = jnp.einsum(
            "qhe,khe->qhk", dattended, block_values, preferred_element_type=jnp.float32
        )
        dscores = (attention * (dprobs - delta[..., None])).astype(jnp.bfloat16)
        grad_query = (
            grad_query
            + jnp.einsum("qhk,khe->qhe", dscores, block_keys, preferred_element_type=jnp.float32)
            * score_scale
        )
        key_part = (
            jnp.einsum("qhk,qhe->khe", dscores, queries, preferred_element_type=jnp.float32)
            * score_scale
        )
        value_part = jnp.einsum(
            "qhk,qhe->khe",
            attention.astype(jnp.bfloat16),
            dattended,
            preferred_element_type=jnp.float32,
        )
        offset = block_index * block_rows
        key_total = lax.dynamic_update_slice_in_dim(key_total, key_part, offset, 0)
        value_total = lax.dynamic_update_slice_in_dim(value_total, value_part, offset, 0)
        return ((grad_query, key_total, value_total), None)

    positions = jnp.arange(blocks[0].shape[0], dtype=jnp.int32)
    state, unused = lax.scan(reflect_advance, grad_start, (positions, blocks))
    grad_query, key_total, value_total = state
    grad_keys, grad_values = (
        lax.psum_scatter(
            key_total.astype(jnp.bfloat16), "ctx", scatter_dimension=0, tiled=True
        ).astype(jnp.float32),
        lax.psum_scatter(
            value_total.astype(jnp.bfloat16), "ctx", scatter_dimension=0, tiled=True
        ).astype(jnp.float32),
    )
    dqkv_low = jnp.concatenate(
        [
            grad_query.reshape(block_len, D),
            grad_keys.reshape(block_len, D),
            grad_values.reshape(block_len, D),
        ],
        1,
    ).astype(jnp.bfloat16)
    grad_bias_query = jnp.sum(dqkv_low[:, :D].astype(jnp.float32), 0)
    grad_bias_value = jnp.sum(dqkv_low[:, 2 * D :].astype(jnp.float32), 0)
    grad_w_qkv = lax.psum_scatter(
        jnp.einsum("td,tc->dc", tokens, dqkv_low, preferred_element_type=jnp.float32).astype(
            jnp.bfloat16
        ),
        "shard",
        scatter_dimension=0,
        tiled=True,
    )
    input_grad = dmixed + jnp.einsum(
        "tc,dc->td", dqkv_low, back_qkv, preferred_element_type=jnp.float32
    )
    smalls = (
        lax.psum_scatter(
            grad_bias_query.astype(jnp.bfloat16), "shard", scatter_dimension=0, tiled=True
        ).astype(jnp.float32),
        lax.psum_scatter(
            grad_bias_value.astype(jnp.bfloat16), "shard", scatter_dimension=0, tiled=True
        ).astype(jnp.float32),
        lax.psum_scatter(
            grad_bias_out.astype(jnp.bfloat16), "shard", scatter_dimension=0, tiled=True
        ).astype(jnp.float32),
        lax.psum_scatter(
            grad_gain_attn.astype(jnp.bfloat16), "shard", scatter_dimension=0, tiled=True
        ).astype(jnp.float32),
        lax.psum_scatter(
            grad_shift_attn.astype(jnp.bfloat16), "shard", scatter_dimension=0, tiled=True
        ).astype(jnp.float32),
        lax.psum_scatter(
            grad_bias_up.astype(jnp.bfloat16), "shard", scatter_dimension=0, tiled=True
        ).astype(jnp.float32),
        lax.psum_scatter(
            grad_bias_down.astype(jnp.bfloat16), "shard", scatter_dimension=0, tiled=True
        ).astype(jnp.float32),
        lax.psum_scatter(
            grad_gain_ffn.astype(jnp.bfloat16), "shard", scatter_dimension=0, tiled=True
        ).astype(jnp.float32),
        lax.psum_scatter(
            grad_shift_ffn.astype(jnp.bfloat16), "shard", scatter_dimension=0, tiled=True
        ).astype(jnp.float32),
    )
    totals = (
        lax.psum(grad_w_qkv, "ctx").astype(jnp.float32),
        lax.psum(smalls[0].astype(jnp.bfloat16), "ctx").astype(jnp.float32),
        lax.psum(smalls[1].astype(jnp.bfloat16), "ctx").astype(jnp.float32),
        lax.psum(grad_w_out, "ctx").astype(jnp.float32),
        lax.psum(smalls[2].astype(jnp.bfloat16), "ctx").astype(jnp.float32),
        lax.psum(smalls[3].astype(jnp.bfloat16), "ctx").astype(jnp.float32),
        lax.psum(smalls[4].astype(jnp.bfloat16), "ctx").astype(jnp.float32),
        lax.psum(grad_w_up, "ctx").astype(jnp.float32),
        lax.psum(smalls[5].astype(jnp.bfloat16), "ctx").astype(jnp.float32),
        lax.psum(grad_w_down, "ctx").astype(jnp.float32),
        lax.psum(smalls[6].astype(jnp.bfloat16), "ctx").astype(jnp.float32),
        lax.psum(smalls[7].astype(jnp.bfloat16), "ctx").astype(jnp.float32),
        lax.psum(smalls[8].astype(jnp.bfloat16), "ctx").astype(jnp.float32),
    )
    return (
        outputs.astype(jnp.bfloat16)[None],
        input_grad[None],
        totals[0],
        totals[1],
        totals[2],
        totals[3],
        totals[4],
        totals[5],
        totals[6],
        totals[7],
        totals[8],
        totals[9],
        totals[10],
        totals[11],
        totals[12],
    )


def solution(mesh):
    return jax.shard_map(
        shards,
        mesh=mesh,
        in_specs=(
            P("shard", "ctx", None),
            P("shard", "ctx", None),
            P("shard", None),
            P("shard"),
            P("shard"),
            P("shard", None),
            P("shard"),
            P("shard"),
            P("shard"),
            P("shard", None),
            P("shard"),
            P("shard", None),
            P("shard"),
            P("shard"),
            P("shard"),
        ),
        out_specs=(
            P("shard", "ctx", None),
            P("shard", "ctx", None),
            P("shard", None),
            P("shard"),
            P("shard"),
            P("shard", None),
            P("shard"),
            P("shard"),
            P("shard"),
            P("shard", None),
            P("shard"),
            P("shard", None),
            P("shard"),
            P("shard"),
            P("shard"),
        ),
        check_vma=False,
    )
```

profile of v0, /device:TPU:6, one launch (start us, length us, event | category | flops | bytes accessed | tf_op | source)
XLA Modules:
  0.0 1131.3 jit_solution(17733610055638063145)
XLA Ops:
  15.8 48.9 %all-reduce.18 = (bf16[1024]{0:T(1024)(128)(2,1)S(1)}, bf16[1024]{0:T(1024)(128)(2,1)S(1)}, bf16[1024]{0:T(1024)(128)(2,1)S(1)}, bf16[1024]{0:T(1024)(128)(2,1)S...) all-reduce(bf16[1024]{0:T(1024)(128)(2,1)S(1)} %dynamic-update-slic, ...), channel_id=1, replica_groups=mesh['ctx'=8,'shard'=16] {'shard'}, use_global_device_ids=true, to_apply=%add.1 | all-reduce | flops 7168 | bytes 28672
  64.8 4.8 fusion.51
  73.7 21.7 %all-gather = bf16[16,1,256]{2,1,0:T(2,128)(2,1)S(1)} all-gather(bf16[1,1,256]{2,1,0:T(2,128)(2,1)S(1)} %reshape.175), channel_id=1, replica_groups=mesh['ctx'=8,'shard'=16] {'shard'}, dimensions={0}, use_global_device_ids=true | all-gather | bytes 8704 | tf_op jit(solution)/shard_map/all_gather | solution.py:75
  95.6 56.7 %all-gather.12.cloned.1.call-done = bf16[2048,16,64]{0,2,1:T(8,128)(2,1)} async-done(((bf16[256,16,64]{0,2,1:T(8,128)(2,1)}), bf16[2048,16,64]{0,2,1:T(8,128)(2,1)}) %all-gather.12.cloned.1.call-update) | async-done | bytes 4194320 | tf_op jit(solution)/shard_map/all_gather | solution.py:113
  152.3 4.8 copy.75
  157.1 69.6 %all-gather.10.cloned.1.call-done = bf16[2048,16,64]{0,2,1:T(8,128)(2,1)} async-done(((bf16[256,16,64]{0,2,1:T(8,128)(2,1)}), bf16[2048,16,64]{0,2,1:T(8,128)(2,1)}) %all-gather.10.cloned.1.call-update) | async-done | bytes 4194320 | tf_op jit(solution)/shard_map/all_gather | solution.py:112
  226.7 4.8 copy.76
  231.5 59.2 %while.30 = (s32[]{:T(128)}, f32[256,16]{0,1:T(8,128)S(1)}, f32[256,16]{0,1:T(8,128)S(1)}, f32[256,16,64]{0,2,1:T(8,128)S(1)}, bf16[4,512,16,64]{1,3,2,0:T(8,128...) while((s32[]{:T(128)}, f32[256,16]{0,1:T(8,128)S(1)}, ...), condition=%wide.region_3.4_spmd.clone, body=%wide.region_0.3_spmd.clone.sunk | while | flops 554455040 | bytes 63702148 | solution.py:136
  231.5 5.8 bitcast_reduce_fusion.2
  237.2 5.0 fusion.129
  243.2 3.0 fusion.131
  246.2 5.8 bitcast_reduce_fusion.2
  252.0 5.0 fusion.129
  257.8 3.0 fusion.131
  260.9 5.8 bitcast_reduce_fusion.2
  266.6 4.9 fusion.129
  272.7 3.0 fusion.131
  275.8 5.8 bitcast_reduce_fusion.2
  281.5 5.1 fusion.129
  287.6 3.0 fusion.131
  290.8 2.7 fusion.83
  294.8 18.9 %all-gather.16.cloned.1.call-done = bf16[1024,4096]{1,0:T(8,128)(2,1)} async-done(((bf16[64,4096]{1,0:T(8,128)(2,1)}), bf16[1024,4096]{1,0:T(8,128)(2,1)}) %all-gather.16.cloned.1.call-update) | async-done | bytes 8388624 | tf_op jit(solution)/shard_map/all_gather | solution.py:74
  313.7 16.5 %multiply_convert_fusion = (bf16[256,4096]{1,0:T(8,128)(2,1)}, f32[256,4096]{1,0:T(8,128)}, f32[256,4096]{1,0:T(8,128)}) fusion(f32[4096]{0:T(1024)S(1)} %bitcast.181, bf16[1024,4096]{1,0:T(8,128)(2,1)} %all-gather.16.cloned.1.call-done, f32[256,1024]{1,0:T(8,128)} %copy-done.2, f32[1024]{0:T(1024)S(1)} %convert_element_type.189, ...), kind=kOutput, calls=%fused_computation.57 | convolution fusion | flops 2218000384 | bytes 19949568 | tf_op jit(solution)/shard_map/dot_general | solution.py:150
  330.2 38.0 %all-gather.18.cloned.1.call-done = bf16[4096,1024]{1,0:T(8,128)(2,1)} async-done(((bf16[256,1024]{1,0:T(8,128)(2,1)}), bf16[4096,1024]{1,0:T(8,128)(2,1)}) %all-gather.18.cloned.1.call-update) | async-done | bytes 8388624 | tf_op jit(solution)/shard_map/all_gather | solution.py:76
  368.2 6.7 fusion.84
  377.9 10.9 fusion.85
  388.9 6.9 multiply_reduce_fusion
  400.1 2.5 broadcast.121
  402.6 2.5 broadcast.121.clone
  405.1 74.6 %while.31 = (s32[]{:T(128)}, f32[256,16,64]{0,2,1:T(8,128)S(1)}, bf16[2048,16,64]{0,2,1:T(8,128)(2,1)}, bf16[2048,16,64]{0,2,1:T(8,128)(2,1)}, bf16[4,512,16,64]...) while((s32[]{:T(128)}, f32[256,16,64]{0,2,1:T(8,128)S(1)}, ...), condition=%wide.region_14.15_spmd.clone, body=%wide.region_13.14_spmd.clone.sunk | while | flops 1360265216 | bytes 99665712 | solution.py:266
  406.5 2.5 fusion.142
  409.1 3.5 fusion.143
  417.9 2.6 bitcast_dynamic-update-slice_fusion.5
  420.5 3.4 fusion.144
  425.1 2.5 fusion.142
  427.7 3.5 fusion.143
  436.5 2.6 bitcast_dynamic-update-slice_fusion.5
  439.1 3.4 fusion.144
  443.7 2.5 fusion.142
  446.3 3.5 fusion.143
  455.1 2.6 bitcast_dynamic-update-slice_fusion.5
  457.7 3.4 fusion.144
  462.3 2.5 fusion.142
  464.9 3.5 fusion.143
  473.7 2.6 bitcast_dynamic-update-slice_fusion.5
  476.3 3.4 fusion.144
  480.7 84.8 %reduce-scatter.9.cloned.1.call-done = bf16[256,16,64]{0,2,1:T(8,128)(2,1)} async-done(((bf16[2048,16,64]{0,2,1:T(8,128)(2,1)}), bf16[256,16,64]{0,2,1:T(8,128)(2,1)}) %reduce-scatter.9.cloned.1.call-update) | async-done | bytes 524304 | tf_op jit(solution)/shard_map/reduce_scatter | solution.py:269
  565.6 87.7 %reduce-scatter.11.cloned.1.call-done = bf16[256,16,64]{0,2,1:T(8,128)(2,1)} async-done(((bf16[2048,16,64]{0,2,1:T(8,128)(2,1)}), bf16[256,16,64]{0,2,1:T(8,128)(2,1)}) %reduce-scatter.11.cloned.1.call-update) | async-done | bytes 524304 | tf_op jit(solution)/shard_map/reduce_scatter | solution.py:272
  653.3 5.7 convert_bitcast_fusion
  659.0 8.7 copy.69
  671.4 7.3 convolution_convert_fusion.1
  679.9 7.2 convolution_convert_fusion
  687.3 53.9 %reduce-scatter.19.cloned.1.call-done = bf16[64,3072]{1,0:T(8,128)(2,1)} async-done(((bf16[1024,3072]{1,0:T(8,128)(2,1)}), bf16[64,3072]{1,0:T(8,128)(2,1)}) %reduce-scatter.19.cloned.1.call-update) | async-done | bytes 393232
  741.2 2.2 copy.70
  743.3 59.6 %reduce-scatter.13.cloned.1.call-done = bf16[64,1024]{1,0:T(8,128)(2,1)} async-done(((bf16[1024,1024]{1,0:T(8,128)(2,1)}), bf16[64,1024]{1,0:T(8,128)(2,1)}) %reduce-scatter.13.cloned.1.call-update) | async-done | bytes 131088 | tf_op jit(solution)/shard_map/reduce_scatter | solution.py:205
  802.9 101.5 %reduce-scatter.15.cloned.1.call-done = bf16[64,4096]{1,0:T(8,128)(2,1)} async-done(((bf16[1024,4096]{1,0:T(8,128)(2,1)}), bf16[64,4096]{1,0:T(8,128)(2,1)}) %reduce-scatter.15.cloned.1.call-update) | async-done | bytes 524304 | tf_op jit(solution)/shard_map/reduce_scatter | solution.py:191
  904.4 99.8 %reduce-scatter.17.cloned.1.call-done = bf16[256,1024]{1,0:T(8,128)(2,1)} async-done(((bf16[4096,1024]{1,0:T(8,128)(2,1)}), bf16[256,1024]{1,0:T(8,128)(2,1)}) %reduce-scatter.17.cloned.1.call-update) | async-done | bytes 524304 | tf_op jit(solution)/shard_map/reduce_scatter | solution.py:175
  1007.3 50.9 %all-reduce.17 = (bf16[1024]{0:T(1024)(128)(2,1)S(1)}, bf16[1024]{0:T(1024)(128)(2,1)S(1)}, bf16[1024]{0:T(1024)(128)(2,1)S(1)}, bf16[1024]{0:T(1024)(128)(2,1)S...) all-reduce(bf16[1024]{0:T(1024)(128)(2,1)S(1)} %dynamic-update-slic, ...), channel_id=1, replica_groups=mesh['ctx'=8,'shard'=16] {'shard'}, use_global_device_ids=true, to_apply=%add.7 | all-reduce | flops 13312 | bytes 53248
  1058.9 25.1 %all-reduce.19 = (bf16[64]{0:T(256)(128)(2,1)S(1)}, bf16[64]{0:T(256)(128)(2,1)S(1)}, bf16[64]{0:T(256)(128)(2,1)S(1)}, bf16[64]{0:T(256)(128)(2,1)S(1)}, bf16[6...) all-reduce(bf16[64]{0:T(256)(128)(2,1)S(1)} %dynamic-slice.9, ...), channel_id=1, replica_groups=mesh['ctx'=8,'shard'=16] {'ctx'}, use_global_device_ids=true, to_apply=%region_21.22 | all-reduce | flops 768 | bytes 3072 | tf_op jit(solution)/shard_map/psum | solution.py:328
  1089.7 6.0 fusion.56
  1095.7 21.6 %all-reduce.23.cloned.1.call-done = (bf16[64,3072]{0,1:T(8,128)(2,1)}, bf16[64,1024]{1,0:T(8,128)(2,1)}, bf16[64,4096]{1,0:T(8,128)(2,1)}, bf16[256,1024]{1,0:T(8,128)(2,1)}) async-done(((bf16[64,3072]{0,1:T(8,128)(2,1)}, bf16[64,1024]{1,0:T(8,128)(2,1)}, bf16[64,4096]{1,0:T(8,128)(2,1)}, bf16[256,1024]{1,0:T(8,128)(2,1)}), (bf16[64,3072]{0,1:T(8,128)(2,1)}, bf16[64,1024]{1,0:T(8,128)(2,1)}, ...) | async-done | bytes 1572880 | tf_op jit(solution)/shard_map/psum | solution.py:327
  1117.3 2.1 convert_element_type.219
  1119.4 2.1 convert_element_type.222
  1121.5 2.3 copy.64
  (203 shorter events, 63.1 us)
Async XLA Ops:
  7.2 57.6 %all-gather.8.cloned.1.call-start = ((), (), s32[]{:S(2)}) async-start(), calls=%async_computation.6 | async-start | bytes 6684672 | tf_op jit(solution)/shard_map/all_gather | solution.py:67
  7.9 144.4 %all-gather.12.cloned.1.call-start = ((), (), s32[]{:S(2)}) async-start(), calls=%async_computation.8 | async-start | bytes 4718592 | tf_op jit(solution)/shard_map/all_gather | solution.py:113
  69.5 4.1 copy-start.23
  70.7 156.0 %all-gather.10.cloned.1.call-start = ((), (), s32[]{:S(2)}) async-start(), calls=%async_computation.7 | async-start | bytes 4718592 | tf_op jit(solution)/shard_map/all_gather | solution.py:112
  71.8 219.0 %all-gather.14.cloned.1.call-start = ((), (), s32[]{:S(2)}) async-start(), calls=%async_computation.9 | async-start | bytes 2228224 | tf_op jit(solution)/shard_map/all_gather | solution.py:70
  72.4 241.3 %all-gather.16.cloned.1.call-start = ((), (), s32[]{:S(2)}) async-start(), calls=%async_computation.10 | async-start | bytes 8912896 | tf_op jit(solution)/shard_map/all_gather | solution.py:74
  73.0 295.3 %all-gather.18.cloned.1.call-start = ((), (), s32[]{:S(2)}) async-start(), calls=%async_computation.11 | async-start | bytes 8912896 | tf_op jit(solution)/shard_map/all_gather | solution.py:76
  73.5 492.0 %reduce-scatter.9.cloned.1.call-start = ((), (), s32[]{:S(2)}) async-start(), calls=%async_computation.12 | async-start | bytes 4718592 | tf_op jit(solution)/shard_map/reduce_scatter | solution.py:269
  237.2 5.9 copy-start
  252.0 5.9 copy-start
  266.6 6.1 copy-start
  281.5 6.1 copy-start
  290.8 39.4 %copy-start.12 = (bf16[256,16,64]{0,2,1:T(8,128)(2,1)}, bf16[256,16,64]{0,2,1:T(8,128)(2,1)S(1)}, u32[]{:S(2)}) copy-start(bf16[256,16,64]{0,2,1:T(8,128)(2,1)S(1)} %fusion.66) | copy-start | bytes 1572868
  293.5 1.0 copy-start.2
  368.2 7.0 copy-start.14
  375.0 1.2 copy-start.7
  375.0 2.9 copy-start.25
  376.2 12.6 %copy-start.16 = (f32[256,1024]{1,0:T(8,128)}, f32[256,1024]{1,0:T(8,128)S(1)}, u32[]{:S(2)}) copy-start(f32[256,1024]{1,0:T(8,128)S(1)} %get-tuple-element.354) | copy-start | bytes 3145732
  377.9 10.9 copy-start.3
  388.8 6.9 copy-start.18
  388.8 8.3 copy-start.11
  396.1 1.0 copy-start.9
  409.1 5.5 copy-start.5
  412.6 1.9 copy-start.1
  415.9 2.0 copy-start.6
  427.7 5.5 copy-start.5
  431.2 1.9 copy-start.1
  434.5 2.0 copy-start.6
  446.2 5.5 copy-start.5
  449.8 1.9 copy-start.1
  453.1 2.0 copy-start.6
  464.8 5.5 copy-start.5
  468.4 1.9 copy-start.1
  471.7 2.0 copy-start.6
  479.7 173.6 %copy-start.19 = (bf16[1,256,1024]{2,1,0:T(8,128)(2,1)S(1)}, bf16[1,256,1024]{2,1,0:T(8,128)(2,1)}, u32[]{:S(2)}) copy-start(bf16[1,256,1024]{2,1,0:T(8,128)(2,1)} %param.19) | copy-start | bytes 1572868
  479.7 173.6 %reduce-scatter.11.cloned.1.call-start = ((), (), s32[]{:S(2)}) async-start(), calls=%async_computation.13 | async-start | bytes 4718592 | tf_op jit(solution)/shard_map/reduce_scatter | solution.py:272
  480.5 260.7 %reduce-scatter.19.cloned.1.call-start = ((), (), s32[]{:S(2)}) async-start(), calls=%async_computation.17 | async-start | bytes 6684672
  480.7 178.2 %copy-start.20 = (bf16[256,16,64]{0,2,1:T(8,128)(2,1)}, bf16[256,16,64]{0,2,1:T(8,128)(2,1)S(1)}, u32[]{:S(2)}) copy-start(bf16[256,16,64]{0,2,1:T(8,128)(2,1)S(1)} %get-tuple-element.358) | copy-start | bytes 1572868
  667.6 1.2 copy-start.10
  667.6 1.4 copy-start.13
  667.7 3.7 copy-start.4
  667.7 135.3 %reduce-scatter.13.cloned.1.call-start = ((), (), s32[]{:S(2)}) async-start(), calls=%async_computation.14 | async-start | bytes 2228224 | tf_op jit(solution)/shard_map/reduce_scatter | solution.py:205
  671.0 233.3 %reduce-scatter.15.cloned.1.call-start = ((), (), s32[]{:S(2)}) async-start(), calls=%async_computation.15 | async-start | bytes 8912896 | tf_op jit(solution)/shard_map/reduce_scatter | solution.py:191
  678.7 1.2 copy-start.17
  678.7 325.5 %reduce-scatter.17.cloned.1.call-start = ((), (), s32[]{:S(2)}) async-start(), calls=%async_computation.16 | async-start | bytes 8912896 | tf_op jit(solution)/shard_map/reduce_scatter | solution.py:175
  687.2 317.1 %copy-start.15 = (bf16[1,256,1024]{2,1,0:T(8,128)(2,1)S(1)}, bf16[1,256,1024]{2,1,0:T(8,128)(2,1)}, u32[]{:S(2)}) copy-start(bf16[1,256,1024]{2,1,0:T(8,128)(2,1)} %param.20) | copy-start | bytes 1572868
  687.2 318.5 %copy-start.24 = (bf16[64]{0:T(256)(128)(2,1)S(1)}, bf16[64]{0:T(256)(128)(2,1)}, u32[]{:S(2)}) copy-start(bf16[64]{0:T(256)(128)(2,1)} %param.33) | copy-start | bytes 388
  687.2 401.5 %copy-start.8 = (f32[256,1024]{1,0:T(8,128)S(1)}, f32[256,1024]{1,0:T(8,128)}, u32[]{:S(2)}) copy-start(f32[256,1024]{1,0:T(8,128)} %copy-done.7) | copy-start | bytes 3145732
  687.2 402.5 %copy-start.21 = (bf16[256,16,64]{0,2,1:T(8,128)(2,1)S(1)}, bf16[256,16,64]{0,2,1:T(8,128)(2,1)}, u32[]{:S(2)}) copy-start(bf16[256,16,64]{0,2,1:T(8,128)(2,1)} %copy-done.20) | copy-start | bytes 1572868
  687.2 430.1 %all-reduce.23.cloned.1.call-start = ((), (), s32[]{:S(2)}) async-start(), calls=%async_computation.18 | async-start | bytes 3932160 | tf_op jit(solution)/shard_map/psum | solution.py:327
  1117.3 6.5 copy-start.22
Sparse Core Ops, SparseCore 0:
  9.7 45.3 all-gather.7
  70.8 81.4 all-gather.11
  155.0 71.6 all-gather.9
  228.3 30.6 all-gather.13
  260.5 53.0 all-gather.15
  315.2 52.9 all-gather.17
  479.8 85.6 reduce-scatter.8
  569.8 83.4 reduce-scatter.10
  667.8 73.3 reduce-scatter.18
  743.4 59.5 reduce-scatter.12
  805.3 98.9 reduce-scatter.14
  906.6 97.5 reduce-scatter.16
  1007.6 109.6 all-reduce.22
where the time goes:
time: 1140 us; the launch traced here: 1130 us
  waiting for transfers between devices  695 us (61%)
  matrix products  167 us (15%)
  blocking collectives  147 us (13%)
  local copies, waits for them, and re-layouts  67.5 us (6%)
  other arithmetic  34.4 us (3%)
  between operations  16.6 us (1%)
    reduce_scatter x1, waiting for transfers between devices, shards(): lax.psum_scatter(jnp.einsum('td,tf->df', first_low, dpre_low, preferred_e...  101 us
    reduce_scatter x1, waiting for transfers between devices, shards(): lax.psum_scatter(jnp.einsum('tf,td->fd', lax.slice_in_dim(activated_low,...  99.8 us
    unnamed x2, blocking collectives  99.8 us
    reduce_scatter x1, waiting for transfers between devices, shards(): lax.psum_scatter(value_total.astype(jnp.bfloat16), 'ctx', scatter_dimensi...  87.7 us
    reduce_scatter x1, waiting for transfers between devices, shards(): lax.psum_scatter(key_total.astype(jnp.bfloat16), 'ctx', scatter_dimension...  84.8 us
    all_gather x1, waiting for transfers between devices, shards(): lax.all_gather(keys, 'ctx', axis=0, tiled=True)  69.6 us
    reduce_scatter x1, waiting for transfers between devices, shards(): lax.psum_scatter(jnp.einsum('td,te->de', attended_low, dattn_low, preferr...  59.6 us
    unnamed x14, waiting for transfers between devices  57 us
  transfers between devices with their start and end apart: 13, of which 11 were waited for; matrix products, arithmetic and copies ran while one was open for 11% of the time, Pallas kernels for 0%

commit v1 on v0

v1 whole, which is shorter than its diff:
```python
from functools import partial

import jax
import jax.numpy as jnp
from jax import lax
from jax.experimental import pallas as pl
from jax.experimental.pallas import tpu as pltpu
from jax.sharding import Mesh, PartitionSpec as P

D = 1024
FF = 4096
HEADS = 16
HD = 64
PAIRS = 8
ROWS = 256
LANES = 128
ln_epsilon = 1e-12
F32 = jnp.float32
BF = jnp.bfloat16

ALL = ("z", "yh", "x", "yl", "core")
SHARD = ("x", "yl", "core")
CTX = ("z", "yh")

NN = (((1,), (0,)), ((), ()))
NT = (((1,), (1,)), ((), ()))
TN = (((0,), (0,)), ((), ()))


def dot(left, right, dims=NN):
    return lax.dot_general(left, right, dims, preferred_element_type=F32)


def place(z, y, x, core):
    return (((z % 4 * 2 + y % 4 // 2) * 4 + x % 4) * 2 + y % 2) * 2 + core % 2


def move(array, dz=0, dy=0, dx=0, dcore=0):
    pairs = [
        (place(z, y, x, core), place(z + dz, y + dy, x + dx, core + dcore))
        for z in range(4)
        for y in range(4)
        for x in range(4)
        for core in range(2)
    ]
    return lax.ppermute(array, ALL, pairs)


def plus(*terms):
    total = terms[0].astype(F32)
    for term in terms[1:]:
        total = total + term.astype(F32)
    return total.astype(BF)


def scatter_sum(sent, kept):
    kept = (
        plus(kept[0], move(sent[0], dy=1)),
        plus(kept[1], move(sent[1], dy=-1)),
    )
    ahead = move(kept[0][2], dx=1)
    behind = move(kept[1][2], dx=-1)
    right = (move(plus(kept[0][1], ahead), dx=1), move(kept[1][1], dx=1))
    left = (move(kept[0][3], dx=-1), move(plus(kept[1][3], behind), dx=-1))
    return tuple(plus(kept[h][0], right[h], left[h]) for h in range(2))


def whole(shape):
    return pl.BlockSpec(shape, lambda *_: (0,) * len(shape))


def project_kernel(x_ref, wq_ref, wk_ref, wv_ref, bq_ref, bv_ref, out_ref):
    x = x_ref[...]
    for part, (w_ref, b_ref) in enumerate(((wq_ref, bq_ref), (wk_ref, None), (wv_ref, bv_ref))):
        value = dot(x, w_ref[...])
        if b_ref is not None:
            value = value + b_ref[...]
        low = value.astype(BF)
        out_ref[0, part] = low[:, :LANES]
        out_ref[1, part] = low[:, LANES:]


def project(x, w_qkv, bias_query, bias_value):
    wide = 2 * LANES
    steps = D // wide

    def block(part):
        return pl.BlockSpec((D, wide), lambda b: (0, part * steps + b))

    bias = pl.BlockSpec((1, wide), lambda b: (0, b))
    return pl.pallas_call(
        project_kernel,
        grid=(steps,),
        in_specs=[whole((ROWS, D)), block(0), block(1), block(2), bias, bias],
        out_specs=pl.BlockSpec((2, 3, ROWS, LANES), lambda b: (b, 0, 0, 0)),
        out_shape=jax.ShapeDtypeStruct((PAIRS, 3, ROWS, LANES), BF),
        compiler_params=pltpu.CompilerParams(vmem_limit_bytes=32 << 20),
        cost_estimate=pl.CostEstimate(
            flops=6 * ROWS * D * D, bytes_accessed=8 * D * D, transcendentals=0
        ),
        name="project",
    )(x, w_qkv, w_qkv, w_qkv, bias_query, bias_value)


def attend_kernel(q_ref, k_ref, v_ref, low_ref, full_ref, lse_ref):
    q = q_ref[...] * jnp.asarray(HD**-0.5, BF)
    k = k_ref[...].reshape(-1, LANES)
    v = v_ref[...].reshape(-1, LANES)
    lane = lax.broadcasted_iota(jnp.int32, q.shape, 1)
    outs, logs = [], []
    for h in range(2):
        mine = (lane < HD) if h == 0 else (lane >= HD)
        scores = dot(jnp.where(mine, q, jnp.zeros_like(q)), k, NT)
        peak = jnp.max(scores, axis=1, keepdims=True)
        expo = jnp.exp(scores - peak)
        total = jnp.sum(expo, axis=1, keepdims=True)
        outs.append(dot(expo.astype(BF), v) / total)
        logs.append(peak + jnp.log(total))
    out = jnp.where(lane < HD, outs[0], outs[1])
    full_ref[...] = out
    low_ref[...] = out.astype(BF)
    lse_ref[...] = jnp.where(lane < HD, logs[0], logs[1])


def part_specs():
    block = pl.BlockSpec((None, None, ROWS, LANES), lambda i: (i, 0, 0, 0))
    keys = pl.BlockSpec((PAIRS, None, ROWS, LANES), lambda i: (0, 1, 0, 0))
    values = pl.BlockSpec((PAIRS, None, ROWS, LANES), lambda i: (0, 2, 0, 0))
    return [block, keys, values]


def attend(qkv):
    rows = pl.BlockSpec((None, ROWS, LANES), lambda i: (i, 0, 0))
    shape = (PAIRS, ROWS, LANES)
    n = PAIRS * ROWS
    return pl.pallas_call(
        attend_kernel,
        grid=(PAIRS,),
        in_specs=part_specs(),
        out_specs=[rows, rows, rows],
        out_shape=[
            jax.ShapeDtypeStruct(shape, BF),
            jax.ShapeDtypeStruct(shape, F32),
            jax.ShapeDtypeStruct(shape, F32),
        ],
        compiler_params=pltpu.CompilerParams(vmem_limit_bytes=48 << 20),
        cost_estimate=pl.CostEstimate(
            flops=16 * n * n * LANES, bytes_accessed=16 * n * LANES, transcendentals=2 * n * n
        ),
        name="attend",
    )(qkv, qkv, qkv)


def reflect_kernel(q_ref, k_ref, v_ref, do_ref, o_ref, lse_ref, out_ref, dk_acc, dv_acc):
    i = pl.program_id(0)

    @pl.when(i == 0)
    def _():
        dk_acc[...] = jnp.zeros_like(dk_acc)
        dv_acc[...] = jnp.zeros_like(dv_acc)

    q = q_ref[...] * jnp.asarray(HD**-0.5, BF)
    do = do_ref[...]
    k = k_ref[...].reshape(-1, LANES)
    v = v_ref[...].reshape(-1, LANES)
    lane = lax.broadcasted_iota(jnp.int32, q.shape, 1)
    product = (do.astype(F32) * o_ref[...]).T
    logs = lse_ref[...].T
    dqs, dk, dv = [], None, None
    for h in range(2):
        mine = (lane < HD) if h == 0 else (lane >= HD)
        qh = jnp.where(mine, q, jnp.zeros_like(q))
        doh = jnp.where(mine, do, jnp.zeros_like(do))
        delta = jnp.sum(product[h * HD : (h + 1) * HD], axis=0, keepdims=True)
        probs = jnp.exp(dot(k, qh, NT) - logs[h * HD : h * HD + 1])
        dscores = (probs * (dot(v, doh, NT) - delta)).astype(BF)
        value_part = dot(probs.astype(BF), doh)
        key_part = dot(dscores, qh)
        dv = value_part if dv is None else dv + value_part
        dk = key_part if dk is None else dk + key_part
        dqs.append(dot(dscores, k, TN))
    dk_acc[...] += dk
    dv_acc[...] += dv
    out_ref[i, 0] = (jnp.where(lane < HD, dqs[0], dqs[1]) * HD**-0.5).astype(BF)

    @pl.when(i == PAIRS - 1)
    def _():
        out_ref[:, 1] = dk_acc[...].astype(BF).reshape(PAIRS, ROWS, LANES)
        out_ref[:, 2] = dv_acc[...].astype(BF).reshape(PAIRS, ROWS, LANES)


def reflect(qkv, dattended, attended, logs):
    rows = pl.BlockSpec((None, ROWS, LANES), lambda i: (i, 0, 0))
    n = PAIRS * ROWS
    return pl.pallas_call(
        reflect_kernel,
        grid=(PAIRS,),
        in_specs=part_specs() + [rows, rows, rows],
        out_specs=whole((PAIRS, 3, ROWS, LANES)),
        out_shape=jax.ShapeDtypeStruct((PAIRS, 3, ROWS, LANES), BF),
        scratch_shapes=[pltpu.VMEM((n, LANES), F32)] * 2,
        compiler_params=pltpu.CompilerParams(vmem_limit_bytes=48 << 20),
        cost_estimate=pl.CostEstimate(
            flops=30 * n * n * LANES, bytes_accessed=20 * n * LANES, transcendentals=2 * n * n
        ),
        name="reflect",
    )(qkv, qkv, qkv, dattended, attended, logs)


ACT, DPRE, FIRST, ATT, DFFN, DATTN = 0, FF, 2 * FF, 2 * FF + D, 2 * FF + 2 * D, 2 * FF + 3 * D
PACKED = 2 * FF + 4 * D
TILE = 512
SMALLS = 6


def normalize(hidden):
    centered = hidden - jnp.mean(hidden, axis=-1, keepdims=True)
    deviation = lax.rsqrt(jnp.mean(centered * centered, axis=-1, keepdims=True) + ln_epsilon)
    return centered * deviation, deviation


def norm_back(upstream, normal, deviation, gain):
    scaled = upstream * gain
    return deviation * (
        scaled
        - jnp.mean(scaled, axis=-1, keepdims=True)
        - normal * jnp.mean(scaled * normal, axis=-1, keepdims=True)
    )


def column_sum(value):
    return jnp.sum(value, axis=0, keepdims=True)


def feed_kernel(
    x_ref, cot_ref, att_ref, vec_ref, bup_ref, wout_hbm, wup_hbm, wdown_hbm,
    out_ref, dmixed_ref, datt_ref, pack_ref,
    wout, wup, wdown, first, normal1, slope, total, sems,
):
    copies = [pltpu.make_async_copy(wout_hbm, wout, sems.at[0])]
    ups, downs = [], []
    for t in range(FF // D):
        cols = pl.ds(t * D, D)
        ups.append(pltpu.make_async_copy(wup_hbm.at[:, cols], wup.at[:, cols], sems.at[1 + 2 * t]))
        downs.append(
            pltpu.make_async_copy(wdown_hbm.at[cols, :], wdown.at[cols, :], sems.at[2 + 2 * t])
        )
    copies[0].start()
    for up, down in zip(ups, downs):
        up.start()
        down.start()

    bias_out, gain1, shift1 = vec_ref[2:3], vec_ref[3:4], vec_ref[4:5]
    bias_down, gain2, shift2 = vec_ref[5:6], vec_ref[6:7], vec_ref[7:8]
    att = jnp.concatenate([att_ref[j] for j in range(PAIRS)], axis=1)
    pack_ref[:ROWS, ATT : ATT + D] = att
    copies[0].wait()
    mixed = x_ref[...].astype(F32) + dot(att, wout[...]) + bias_out
    n1, r1 = normalize(mixed)
    normal1[...] = n1
    value = n1 * gain1 + shift1
    first[...] = value
    first_low = value.astype(BF)
    pack_ref[:ROWS, FIRST : FIRST + D] = first_low

    total[...] = value + bias_down
    for t in range(FF // D):
        ups[t].wait()
        downs[t].wait()

        @pl.loop(0, D // TILE)
        def _(u):
            cols = pl.ds(pl.multiple_of(t * D + u * TILE, TILE), TILE)
            pre = dot(pack_ref[:ROWS, FIRST : FIRST + D], wup[:, cols]) + bup_ref[:, cols]
            cdf = 0.5 * (1.0 + lax.erf(pre * 0.7071067811865476))
            slope[:, cols] = cdf + pre * (jnp.exp(-0.5 * pre * pre) * 0.3989422804014327)
            act = (pre * cdf).astype(BF)
            pack_ref[:ROWS, cols] = act
            total[...] += dot(act, wdown[cols, :])

    n2, r2 = normalize(total[...])
    out_ref[...] = (n2 * gain2 + shift2).astype(BF)
    dy = cot_ref[...].astype(F32)
    sums = [None] * SMALLS
    sums[4] = column_sum(dy * n2)
    sums[5] = column_sum(dy)
    dffn = norm_back(dy, n2, r2, gain2)
    dffn_low = dffn.astype(BF)
    pack_ref[:ROWS, DFFN : DFFN + D] = dffn_low
    sums[3] = column_sum(dffn_low.astype(F32))
    total[...] = dffn
    pack_ref[ROWS:, :] = jnp.zeros((16, PACKED), BF)

    @pl.loop(0, FF // TILE)
    def _(u):
        cols = pl.ds(pl.multiple_of(u * TILE, TILE), TILE)
        grads = dot(pack_ref[:ROWS, DFFN : DFFN + D], wdown[cols, :], NT) * slope[:, cols]
        low = grads.astype(BF)
        pack_ref[:ROWS, pl.ds(pl.multiple_of(DPRE + u * TILE, TILE), TILE)] = low
        pack_ref[ROWS:, cols] = jnp.broadcast_to(column_sum(low.astype(F32)), (16, TILE)).astype(BF)
        total[...] += dot(low, wup[:, cols], NT)

    dfirst = total[...]
    n1 = normal1[...]
    sums[1] = column_sum(dfirst * n1)
    sums[2] = column_sum(dfirst)
    dmixed = norm_back(dfirst, n1, r1, gain1)
    dmixed_ref[...] = dmixed
    low = dmixed.astype(BF)
    pack_ref[:ROWS, DATTN : DATTN + D] = low
    sums[0] = column_sum(low.astype(F32))
    for row, value in enumerate(sums):
        pack_ref[ROWS:, FF + row * D : FF + (row + 1) * D] = jnp.broadcast_to(
            value, (16, D)
        ).astype(BF)
    datt = dot(low, wout[...], NT).astype(BF)
    for j in range(PAIRS):
        datt_ref[j] = datt[:, j * LANES : (j + 1) * LANES]


def feed(x, cotangent, attended, vectors, bias_up, w_out, w_up, w_down):
    vmem = pl.BlockSpec(memory_space=pltpu.VMEM)
    hbm = pl.BlockSpec(memory_space=pl.ANY)
    return pl.pallas_call(
        feed_kernel,
        in_specs=[vmem] * 5 + [hbm] * 3,
        out_specs=[vmem] * 4,
        out_shape=[
            jax.ShapeDtypeStruct((ROWS, D), BF),
            jax.ShapeDtypeStruct((ROWS, D), F32),
            jax.ShapeDtypeStruct((PAIRS, ROWS, LANES), BF),
            jax.ShapeDtypeStruct((ROWS + 16, PACKED), BF),
        ],
        scratch_shapes=[
            pltpu.VMEM((D, D), BF),
            pltpu.VMEM((D, FF), BF),
            pltpu.VMEM((FF, D), BF),
            pltpu.VMEM((ROWS, D), F32),
            pltpu.VMEM((ROWS, D), F32),
            pltpu.VMEM((ROWS, FF), F32),
            pltpu.VMEM((ROWS, D), F32),
            pltpu.SemaphoreType.DMA((9,)),
        ],
        compiler_params=pltpu.CompilerParams(vmem_limit_bytes=56 << 20),
        cost_estimate=pl.CostEstimate(
            flops=40 * ROWS * D * D, bytes_accessed=32 * D * D, transcendentals=2 * ROWS * FF
        ),
        name="feed",
    )(x, cotangent, attended, vectors, bias_up, w_out, w_up, w_down)


def pick(ref, base, slot, group):
    block = ref[:, pl.ds(pl.multiple_of(base + slot * 256, 256), 256)]
    out = block[:, :HD]
    for g in range(1, 4):
        out = jnp.where(group == g, block[:, g * HD : (g + 1) * HD], out)
    return out


def pick_all(ref, base, where_x, group):
    return jnp.concatenate(
        [pick(ref, base, lax.rem(where_x + d, 4), group) for d in range(4)], axis=1
    )


HALF_A = 160
HALF_B = 144
HALF_C = 112


def grads_a_kernel(at_ref, own_ref, far_ref, one_ref, two_ref):
    where_x, group = at_ref[0], at_ref[1]

    def product(left, right):
        return dot(left(own_ref), own_ref[:ROWS, right : right + D], TN) + dot(
            left(far_ref), far_ref[:ROWS, right : right + D], TN
        )

    for d in range(4):
        slot = lax.rem(where_x + d, 4) * 4 + group
        value = product(
            lambda ref: ref[:ROWS, pl.ds(pl.multiple_of(slot * 256, 256), 256)], DFFN
        ).astype(BF)
        one_ref[d, :128] = value[:128]
        two_ref[d, :128] = value[128:]
    value = product(
        lambda ref: pick_all(ref.at[:ROWS], ATT, where_x, group), DATTN
    ).astype(BF)
    for d in range(4):
        one_ref[d, 128:160] = value[d * 64 : d * 64 + 32]
        two_ref[d, 128:160] = value[d * 64 + 32 : d * 64 + 64]


def grads_b_kernel(at_ref, own_ref, far_ref, one_ref, two_ref):
    where_x, group = at_ref[0], at_ref[1]
    own = pick_all(own_ref.at[:ROWS], FIRST, where_x, group)
    far = pick_all(far_ref.at[:ROWS], FIRST, where_x, group)
    for block in range(FF // D):
        cols = slice(DPRE + block * D, DPRE + (block + 1) * D)
        value = (
            dot(own, own_ref[:ROWS, cols], TN) + dot(far, far_ref[:ROWS, cols], TN)
        ).astype(BF)
        target = (one_ref, two_ref)[block // 2]
        start = block % 2 * 64
        for d in range(4):
            target[d, start : start + 64] = value[d * 64 : (d + 1) * 64]
    row = lax.broadcasted_iota(jnp.int32, (16, D), 0)
    for d in range(4):
        slot = lax.rem(where_x + d, 4)
        tail = jnp.zeros((16, D), F32)
        cols = pl.ds(pl.multiple_of((slot * 4 + group) * 256, 256), 256)
        for ref in (own_ref, far_ref):
            parts = [ref[ROWS:, cols].astype(F32)]
            for k in range(SMALLS):
                parts.append(pick(ref.at[ROWS:], FF + k * D, slot, group).astype(F32))
            parts.append(jnp.zeros((16, D - 256 - SMALLS * HD), F32))
            tail = tail + jnp.concatenate(parts, axis=1)
        one_ref[d, 128:144] = jnp.where(row == 0, tail, 0.0).astype(BF)
        two_ref[d, 128:144] = jnp.zeros((16, D), BF)


def grads_c_kernel(at_ref, own_x_ref, far_x_ref, own_ref, far_ref, one_ref, two_ref):
    where_x, group = at_ref[0], at_ref[1]
    own = pick_all(own_x_ref, 0, where_x, group)
    far = pick_all(far_x_ref, 0, where_x, group)
    bias = []
    values = []
    for part in range(3):
        mine = jnp.concatenate([own_ref[j, part] for j in range(PAIRS)], axis=1)
        other = jnp.concatenate([far_ref[j, part] for j in range(PAIRS)], axis=1)
        values.append((dot(own, mine, TN) + dot(far, other, TN)).astype(BF))
        if part != 1:
            bias.append(column_sum(mine.astype(F32)) + column_sum(other.astype(F32)))
    row = lax.broadcasted_iota(jnp.int32, (16, D), 0)
    for d in range(4):
        rows = slice(d * 64, (d + 1) * 64)
        low = slice(d * 64, d * 64 + 32)
        high = slice(d * 64 + 32, (d + 1) * 64)
        one_ref[d, :64] = values[0][rows]
        one_ref[d, 64:96] = values[1][low]
        one_ref[d, 96:112] = jnp.zeros((16, D), BF)
        two_ref[d, :32] = values[1][high]
        two_ref[d, 32:96] = values[2][rows]
        slot = lax.rem(where_x + d, 4)
        parts = []
        for vector in bias:
            out = jnp.zeros((1, HD), F32)
            for s in range(16):
                out = jnp.where(slot * 4 + group == s, vector[:, s * HD : (s + 1) * HD], out)
            parts.append(out)
        parts.append(jnp.zeros((1, D - 2 * HD), F32))
        tail = jnp.broadcast_to(jnp.concatenate(parts, axis=1), (16, D))
        two_ref[d, 96:112] = jnp.where(row == 0, tail, 0.0).astype(BF)


def grads(kernel, half, name, flops, at, *arrays):
    vmem = pl.BlockSpec(memory_space=pltpu.VMEM)
    shape = jax.ShapeDtypeStruct((4, half, D), BF)
    return pl.pallas_call(
        kernel,
        in_specs=[pl.BlockSpec(memory_space=pltpu.SMEM)] + [vmem] * len(arrays),
        out_specs=[vmem, vmem],
        out_shape=[shape, shape],
        compiler_params=pltpu.CompilerParams(vmem_limit_bytes=48 << 20),
        cost_estimate=pl.CostEstimate(flops=flops, bytes_accessed=20 << 20, transcendentals=0),
        name=name,
    )(at, *arrays)


def return_kernel(dmixed_ref, grad_ref, w_ref, out_ref):
    step = pl.program_id(0)
    both = jnp.concatenate([grad_ref[0], grad_ref[1]], axis=1)
    value = dot(both, w_ref[...], NT)

    @pl.when(step == 0)
    def _():
        out_ref[...] = dmixed_ref[...] + value

    @pl.when(step > 0)
    def _():
        out_ref[...] += value


def return_input(dmixed, dqkv, w_qkv):
    wide = 2 * LANES
    steps = D // wide
    return pl.pallas_call(
        return_kernel,
        grid=(3 * steps,),
        in_specs=[
            whole((ROWS, D)),
            pl.BlockSpec((2, None, ROWS, LANES), lambda i: (i % steps, i // steps, 0, 0)),
            pl.BlockSpec((D, wide), lambda i: (0, i)),
        ],
        out_specs=whole((ROWS, D)),
        out_shape=jax.ShapeDtypeStruct((ROWS, D), F32),
        compiler_params=pltpu.CompilerParams(vmem_limit_bytes=32 << 20),
        cost_estimate=pl.CostEstimate(
            flops=6 * ROWS * D * D, bytes_accessed=8 * D * D, transcendentals=0
        ),
        name="return_input",
    )(dmixed, dqkv, w_qkv)


def gather(array):
    return lax.all_gather(array, SHARD, axis=0, tiled=True)


def exchange(array):
    return lax.all_to_all(array, CTX, 0, 0, tiled=True)


def shards(
    inputs, cotangent, w_qkv, bias_query, bias_value, w_out, bias_out, gain_attn, shift_attn,
    w_up, bias_up, w_down, bias_down, gain_ffn, shift_ffn,
):
    tokens = inputs[0]
    where_x = lax.axis_index("x").astype(jnp.int32)
    where_y = lax.axis_index("yl").astype(jnp.int32)
    core = lax.axis_index("core").astype(jnp.int32)
    own = jnp.stack([where_x, where_y * 2 + core])
    other = jnp.stack([where_x, (1 - where_y) * 2 + core])

    small = jnp.concatenate(
        [bias_query, bias_value, bias_out, gain_attn, shift_attn, bias_down, gain_ffn, shift_ffn,
         bias_up, jnp.zeros((256,), BF)]
    ).reshape(8, LANES)
    full_small = gather(small).reshape(16, 8 * LANES)
    full_qkv = gather(w_qkv)
    vectors = (
        full_small[:, : 8 * HD].reshape(16, 8, HD).transpose(1, 0, 2).reshape(8, D).astype(F32)
    )
    full_bias_up = full_small[:, 8 * HD : 8 * HD + 256].reshape(1, FF).astype(F32)
    far_tokens = move(tokens, dcore=1)

    qkv = exchange(project(tokens, full_qkv, vectors[0:1], vectors[1:2]))
    full_out = gather(w_out)
    full_up = gather(w_up)
    full_down = gather(w_down)
    attended_low, attended, logs = attend(qkv)
    attended_low = exchange(attended_low)
    outputs, dmixed, dattended, pack = feed(
        tokens, cotangent[0], attended_low, vectors, full_bias_up, full_out, full_up, full_down
    )
    far_pack = move(pack, dcore=1)
    dattended = exchange(dattended)

    flops = 4 * ROWS * D * 2 * D
    sent_a = grads(grads_a_kernel, HALF_A, "grads_a", flops, other, pack, far_pack)
    sent_b = grads(grads_b_kernel, HALF_B, "grads_b", flops, other, pack, far_pack)
    kept_a = grads(grads_a_kernel, HALF_A, "grads_a", flops, own, pack, far_pack)
    kept_b = grads(grads_b_kernel, HALF_B, "grads_b", flops, own, pack, far_pack)
    summed_a = scatter_sum(sent_a, kept_a)
    summed_b = scatter_sum(sent_b, kept_b)

    dqkv = reflect(qkv, dattended, attended, logs)
    dqkv = exchange(dqkv)
    far_dqkv = move(dqkv, dcore=1)
    args = (tokens, far_tokens, dqkv, far_dqkv)
    sent_c = grads(grads_c_kernel, HALF_C, "grads_c", flops, other, *args)
    kept_c = grads(grads_c_kernel, HALF_C, "grads_c", flops, own, *args)
    input_grad = return_input(dmixed, dqkv, full_qkv)
    summed_c = scatter_sum(sent_c, kept_c)

    first_sum = lax.psum_scatter(
        jnp.concatenate(summed_a + summed_b, axis=0), CTX, scatter_dimension=0, tiled=True
    )
    first_sum = lax.all_gather(first_sum, CTX, axis=0, tiled=True).astype(F32)
    last = jnp.concatenate(summed_c, axis=0).reshape(PAIRS, 2 * HALF_C // PAIRS, D)
    last = exchange(last)
    last = jnp.sum(last.astype(F32), axis=0).astype(BF)
    last = lax.all_gather(last, CTX, axis=0, tiled=True).astype(F32)

    a1, a2 = first_sum[:HALF_A], first_sum[HALF_A : 2 * HALF_A]
    b = first_sum[2 * HALF_A :]
    b1, b2 = b[:HALF_B], b[HALF_B:]
    grad_down = jnp.concatenate([a1[:128], a2[:128]], axis=0)
    grad_out = jnp.concatenate([a1[128:160], a2[128:160]], axis=0)
    grad_up = jnp.concatenate([b1[:64], b1[64:128], b2[:64], b2[64:128]], axis=1)
    row = b1[128]
    grad_bias_up = row[:256]
    smalls = [row[256 + k * HD : 256 + (k + 1) * HD] for k in range(SMALLS)]
    c1, c2 = last[:HALF_C], last[HALF_C:]
    grad_qkv = jnp.concatenate(
        [c1[:64], jnp.concatenate([c1[64:96], c2[:32]], axis=0), c2[32:96]], axis=1
    )
    return (
        outputs[None],
        input_grad[None],
        grad_qkv,
        c2[96, :HD],
        c2[96, HD : 2 * HD],
        grad_out,
        smalls[0],
        smalls[1],
        smalls[2],
        grad_up,
        grad_bias_up,
        grad_down,
        smalls[3],
        smalls[4],
        smalls[5],
    )


def solution(mesh):
    fine = Mesh(mesh.devices.reshape(4, 2, 4, 2, 2), ALL)
    tokens = P(SHARD, CTX, None)
    matrix = P(SHARD, None)
    vector = P(SHARD)
    parameters = (
        matrix, vector, vector, matrix, vector, vector, vector,
        matrix, vector, matrix, vector, vector, vector,
    )
    return jax.shard_map(
        shards,
        mesh=fine,
        in_specs=(tokens, tokens) + parameters,
        out_specs=(tokens, tokens) + parameters,
        check_vma=False,
    )
```

time: 1140 us -> 572 us (0.50)
  waiting for transfers between devices: 695 us -> 190 us
  matrix products: 167 us -> 0 us
  Pallas kernels: 0 us -> 107 us
  local copies, waits for them, and re-layouts: 67.5 us -> 21.4 us
  starting transfers between devices: 0.77 us -> 44 us
  blocking collectives: 147 us -> 169 us
  other arithmetic: 34.4 us -> 15.6 us
    reduce_scatter x5 -> x0, waiting for transfers between devices: 433 us -> none  [the longest x1 101 us: shards(): lax.psum_scatter(jnp.einsum('td,tf->df', first_low, dpre_low, preferred_e...]
    dot_general x40 -> x0, matrix products: 167 us -> none  [the longest x4 23.1 us: absorb_advance(): jnp.einsum('qhe,khe->qhk', queries, block_keys, preferred_element_type=jn...]
    pallas_call x0 -> x11, Pallas kernels: none -> 107 us  [the longest x6 34.1 us: grads(): pl.pallas_call(kernel, in_specs=[pl.BlockSpec(memory_space=pltpu.SMEM)] +...]
    all_gather x6 -> x5, waiting for transfers between devices: 183 us -> 97.5 us  [the longest x4 97.5 us: gather(): return lax.all_gather(array, SHARD, axis=0, tiled=True)]
    all_to_all x0 -> x3, blocking collectives: none -> 82.4 us  [exchange(): return lax.all_to_all(array, CTX, 0, 0, tiled=True)]
    ppermute x0 -> x27, waiting for transfers between devices: none -> 71.1 us  [move(): return lax.ppermute(array, ALL, pairs)]
    unnamed x2 -> x1, blocking collectives: 99.8 us -> 32.8 us
    unnamed x14 -> x6, waiting for transfers between devices: 57 us -> 3.88 us
  transfers between devices with their start and end apart: 13 -> 35, of which waited for: 11 -> 18; matrix products, arithmetic and copies ran while one was open for 11% -> 9% of each run, Pallas kernels for 0% -> 15%
where the time goes in v1:
time: 572 us; the launch traced here: 563 us
  waiting for transfers between devices  190 us (33%)
  blocking collectives  169 us (30%)
  Pallas kernels  107 us (19%)
  starting transfers between devices  44 us (8%)
  local copies, waits for them, and re-layouts  21.4 us (4%)
  other arithmetic  15.6 us (3%)
  between operations  15.6 us (3%)
    all_gather x4, waiting for transfers between devices, gather(): return lax.all_gather(array, SHARD, axis=0, tiled=True)  97.5 us
    all_to_all x3, blocking collectives, exchange(): return lax.all_to_all(array, CTX, 0, 0, tiled=True)  82.4 us
    ppermute x27, waiting for transfers between devices, move(): return lax.ppermute(array, ALL, pairs)  71.1 us
    all_gather x1, blocking collectives, shards(): last = lax.all_gather(last, CTX, axis=0, tiled=True).astype(F32)  37.4 us
    pallas_call x6, Pallas kernels, grads(): pl.pallas_call(kernel, in_specs=[pl.BlockSpec(memory_space=pltpu.SMEM)] +...  34.1 us
    ppermute x27, starting transfers between devices, move(): return lax.ppermute(array, ALL, pairs)  33.2 us
    unnamed x1, blocking collectives  32.8 us
    pallas_call x1, Pallas kernels, reflect(): pl.pallas_call(reflect_kernel, grid=(PAIRS,), in_specs=part_specs() + [ro...  23.8 us
  transfers between devices with their start and end apart: 35, of which 18 were waited for; matrix products, arithmetic and copies ran while one was open for 9% of the time, Pallas kernels for 15%

profile of v1, /device:TPU:6, one launch (start us, length us, event | category | flops | bytes accessed | tf_op | source)
XLA Modules:
  0.0 563.1 jit_solution(16943293834881653479)
XLA Ops:
  10.3 16.4 %all_gather.22 = bf16[128,128]{1,0:T(8,128)(2,1)S(1)} all-gather(bf16[8,128]{1,0:T(8,128)(2,1)S(1)} %bitcast.132), channel_id=1, replica_groups=mesh['z'=4,'yh'=2,'x'=4,'yl'=2,'core'=2] {'x','yl','core'}, dimensions={0}, use_global_device_ids=true | all-gather | bytes 34816 | tf_op jit(solution)/shard_map/all_gather | solution.py:506
  27.0 27.3 %all-gather.8.cloned.1.call-done.wq_ref.wk_ref.wv_ref.w_ref = bf16[1024,3072]{1,0:T(8,128)(2,1)} async-done(((bf16[64,3072]{1,0:T(8,128)(2,1)}), bf16[1024,3072]{1,0:T(8,128)(2,1)}) %all-gather.8.cloned.1.call-update) | async-done | bytes 6291472 | tf_op jit(solution)/shard_map/all_gather | solution.py:506
  54.4 2.8 copy-done
  57.1 3.2 project.1
  60.4 38.3 %all_to_all.25.q_ref.k_ref.v_ref = bf16[8,3,256,128]{3,2,1,0:T(8,128)(2,1)S(1)} all-to-all(bf16[8,3,256,128]{3,2,1,0:T(8,128)(2,1)S(1)} %project.1), channel_id=1, replica_groups=mesh['z'=4,'yh'=2,'x'=4,'yl'=2,'core'=2] {'z','yh'}, dimensions={0} | all-to-all | bytes 3145728 | tf_op jit(solution)/shard_map/all_to_all | solution.py:510
  98.7 15.2 %attend.1 = (bf16[8,256,128]{2,1,0:T(8,128)(2,1)}, f32[8,256,128]{2,1,0:T(8,128)S(1)}, f32[8,256,128]{2,1,0:T(8,128)S(1)}) custom-call(bf16[8,3,256,128]{3,2,1,0:T(8,128)(2,1)S(1)} %all_to_all.25.q_ref.k_ref.v_ref, bf16[8,3,256,128]{3,2,1,0:T(8,128)(2,1)S(1)} %all_to_all.25.q_ref.k_ref.v_ref, bf16[8,3,256,128]{3,2,1,0:T(8,128)(2,1)S(1)} %all_to_all.25.q_ref.k_ref.v_ref), custom_call_target="tpu_custom_call" | custom-call | flops 8589934592 | bytes 4194304 | tf_op jit(solution)/shard_map/attend/pallas_call | solution.py:136
  113.9 1.0 copy-done.5
  114.8 3.5 all-to-all-start.1
  119.7 16.7 %all-to-all-done.1.att_ref = bf16[8,256,128]{2,1,0:T(8,128)(2,1)S(1)} async-done(((bf16[8,256,128]{2,1,0:T(8,128)(2,1)}), bf16[8,256,128]{2,1,0:T(8,128)(2,1)S(1)}, u32[]{:S(2)}, u32[]{:S(2)}) %all-to-all-start.1) | async-done | bytes 524320 | tf_op jit(solution)/shard_map/all_to_all | solution.py:510
  136.4 15.9 %all-gather.12.cloned.1.call-done.wup_hbm = bf16[1024,4096]{1,0:T(8,128)(2,1)} async-done(((bf16[64,4096]{1,0:T(8,128)(2,1)}), bf16[1024,4096]{1,0:T(8,128)(2,1)}) %all-gather.12.cloned.1.call-update) | async-done | bytes 8388624 | tf_op jit(solution)/shard_map/all_gather | solution.py:506
  152.2 54.3 %all-gather.14.cloned.1.call-done.wdown_hbm = bf16[4096,1024]{1,0:T(8,128)(2,1)} async-done(((bf16[256,1024]{1,0:T(8,128)(2,1)}), bf16[4096,1024]{1,0:T(8,128)(2,1)}) %all-gather.14.cloned.1.call-update) | async-done | bytes 8388624 | tf_op jit(solution)/shard_map/all_gather | solution.py:506
  206.5 23.5 %feed.1 = (bf16[256,1024]{1,0:T(8,128)(2,1)}, f32[256,1024]{1,0:T(8,128)}, bf16[8,256,128]{2,1,0:T(8,128)(2,1)}, bf16[272,12288]{1,0:T(8,128)(2,1)}) custom-call(bf16[256,1024]{1,0:T(8,128)(2,1)} %bitcast.122, bf16[256,1024]{1,0:T(8,128)(2,1)} %bitcast.134, bf16[8,256,128]{2,1,0:T(8,128)(2,1)} %copy-done.9, f32[8,1024]{1,0:T(8,128)} %convert_element_type.241.vec_ref, ...), custom_call_target="tpu_custom_call" | custom-call | flops 10737418240 | bytes 33554432 | tf_op jit(solution)/shard_map/feed/pallas_call | solution.py:324
  230.3 18.8 %all_to_all.26.do_ref = bf16[8,256,128]{2,1,0:T(8,128)(2,1)S(1)} all-to-all(bf16[8,256,128]{2,1,0:T(8,128)(2,1)} %get-tuple-element.37), channel_id=1, replica_groups=mesh['z'=4,'yh'=2,'x'=4,'yl'=2,'core'=2] {'z','yh'}, dimensions={0} | all-to-all | bytes 1048576 | tf_op jit(solution)/shard_map/all_to_all | solution.py:510
  249.1 23.8 %reflect.1 = bf16[8,3,256,128]{3,2,1,0:T(8,128)(2,1)S(1)} custom-call(bf16[8,3,256,128]{3,2,1,0:T(8,128)(2,1)S(1)} %all_to_all.25.q_ref.k_ref.v_ref, bf16[8,3,256,128]{3,2,1,0:T(8,128)(2,1)S(1)} %all_to_all.25.q_ref.k_ref.v_ref, bf16[8,3,256,128]{3,2,1,0:T(8,128)(2,1)S(1)} %all_to_all.25.q_ref.k_ref.v_ref, bf16[8,256,128]{2,1,0:T(8,128)(2,1)S(1)} %all_to_all.26.do_ref, ...), custom_call_target="tpu_custom_call" | custom-call | flops 16106127360 | bytes 5242880 | tf_op jit(solution)/shard_map/reflect/pallas_call | solution.py:195
  272.9 25.4 %all_to_all.27.grad_ref.own_ref = bf16[8,3,256,128]{3,2,1,0:T(8,128)(2,1)S(1)} all-to-all(bf16[8,3,256,128]{3,2,1,0:T(8,128)(2,1)S(1)} %reflect.1), channel_id=1, replica_groups=mesh['z'=4,'yh'=2,'x'=4,'yl'=2,'core'=2] {'z','yh'}, dimensions={0} | all-to-all | bytes 3145728 | tf_op jit(solution)/shard_map/all_to_all | solution.py:510
  298.9 3.2 collective-permute-done.far_x_ref
  302.6 4.2 grads_c.3
  308.6 2.8 collective-permute-start.6
  311.4 3.5 grads_c.2
  314.9 15.9 %collective-permute-done.2 = bf16[4,112,1024]{2,1,0:T(8,128)(2,1)} collective-permute-done((bf16[4,112,1024]{2,1,0:T(8,128)(2,1)}, bf16[4,112,1024]{2,1,0:T(8,128)(2,1)}, u32[]{:S(2)}, u32[]{:S(2)}) %collective-permute-start.2) | collective-permute-done | bytes 917536 | tf_op jit(solution)/shard_map/ppermute | solution.py:46
  330.8 1.5 add_convert_fusion.5
  333.9 1.2 collective-permute-start.5
  335.1 6.8 %grads_b.3 = (bf16[4,144,1024]{2,1,0:T(8,128)(2,1)S(1)}, bf16[4,144,1024]{2,1,0:T(8,128)(2,1)S(1)}) custom-call(s32[2]{0:T(128)S(1)} %get-tuple-element.88.at_ref, bf16[272,12288]{1,0:T(8,128)(2,1)} %get-tuple-element.44.own_ref, bf16[272,12288]{1,0:T(8,128)(2,1)} %collective-permute-done.10.far_ref), custom_call_target="tpu_custom_call" | custom-call | flops 2147483648 | bytes 20971520 | tf_op jit(solution)/shard_map/grads_b/pallas_call | solution.py:459
  342.4 3.5 collective-permute-start.23
  346.6 6.5 %grads_a.3 = (bf16[4,160,1024]{2,1,0:T(8,128)(2,1)S(1)}, bf16[4,160,1024]{2,1,0:T(8,128)(2,1)S(1)}) custom-call(s32[2]{0:T(128)S(1)} %get-tuple-element.88.at_ref, bf16[272,12288]{1,0:T(8,128)(2,1)} %get-tuple-element.44.own_ref, bf16[272,12288]{1,0:T(8,128)(2,1)} %collective-permute-done.10.far_ref), custom_call_target="tpu_custom_call" | custom-call | flops 2147483648 | bytes 20971520 | tf_op jit(solution)/shard_map/grads_a/pallas_call | solution.py:459
  353.2 3.2 collective-permute-start.15
  356.4 6.5 %grads_a.2 = (bf16[4,160,1024]{2,1,0:T(8,128)(2,1)S(1)}, bf16[4,160,1024]{2,1,0:T(8,128)(2,1)S(1)}) custom-call(s32[2]{0:T(128)S(1)} %get-tuple-element.87.at_ref, bf16[272,12288]{1,0:T(8,128)(2,1)} %get-tuple-element.44.own_ref, bf16[272,12288]{1,0:T(8,128)(2,1)} %collective-permute-done.10.far_ref), custom_call_target="tpu_custom_call" | custom-call | flops 2147483648 | bytes 20971520 | tf_op jit(solution)/shard_map/grads_a/pallas_call | solution.py:459
  362.9 6.8 %grads_b.2 = (bf16[4,144,1024]{2,1,0:T(8,128)(2,1)S(1)}, bf16[4,144,1024]{2,1,0:T(8,128)(2,1)S(1)}) custom-call(s32[2]{0:T(128)S(1)} %get-tuple-element.87.at_ref, bf16[272,12288]{1,0:T(8,128)(2,1)} %get-tuple-element.44.own_ref, bf16[272,12288]{1,0:T(8,128)(2,1)} %collective-permute-done.10.far_ref), custom_call_target="tpu_custom_call" | custom-call | flops 2147483648 | bytes 20971520 | tf_op jit(solution)/shard_map/grads_b/pallas_call | solution.py:459
  369.7 2.5 collective-permute-done.19
  372.2 1.7 add_convert_fusion.3
  373.9 2.1 collective-permute-start.20
  376.0 1.7 add_convert_fusion.2
  377.8 20.0 %collective-permute-done.11 = bf16[4,160,1024]{2,1,0:T(8,128)(2,1)S(1)} collective-permute-done((bf16[4,160,1024]{2,1,0:T(8,128)(2,1)S(1)}, bf16[4,160,1024]{2,1,0:T(8,128)(2,1)S(1)}, u32[]{:S(2)}, u32[]{:S(2)}) %collective-permute-start.11) | collective-permute-done | bytes 1310752 | tf_op jit(solution)/shard_map/ppermute | solution.py:46
  399.2 2.5 collective-permute-start.24
  403.3 2.5 collective-permute-done.25
  405.9 7.6 %collective-permute-done.12 = bf16[160,1024]{1,0:T(8,128)(2,1)S(1)} collective-permute-done((bf16[160,1024]{1,0:T(8,128)(2,1)S(1)}, bf16[160,1024]{1,0:T(8,128)(2,1)S(1)}, u32[]{:S(2)}, u32[]{:S(2)}) %collective-permute-start.12) | collective-permute-done | bytes 327712 | tf_op jit(solution)/shard_map/ppermute | solution.py:46
  413.5 2.9 collective-permute-start.21
  416.8 4.4 collective-permute-done.21
  421.2 3.8 collective-permute-start.13
  425.2 2.5 collective-permute-done.26
  427.9 6.9 %collective-permute-done.14 = bf16[160,1024]{1,0:T(8,128)(2,1)S(1)} collective-permute-done((bf16[160,1024]{1,0:T(8,128)(2,1)S(1)}, bf16[160,1024]{1,0:T(8,128)(2,1)S(1)}, u32[]{:S(2)}, u32[]{:S(2)}) %collective-permute-start.14) | collective-permute-done | bytes 327712 | tf_op jit(solution)/shard_map/ppermute | solution.py:46
  434.7 3.2 collective-permute-start.7
  438.1 1.4 collective-permute-done.16
  439.6 3.7 collective-permute-start.4
  443.5 32.8 %fusion = bf16[80,1024]{1,0:T(8,128)(2,1)S(1)} fusion(bf16[608,1024]{1,0:T(8,128)(2,1)S(1)} %pad_maximum_fusion), kind=kCustom, calls=%all-reduce-scatter | all-reduce-scatter fusion | flops 655361 | bytes 1409536
  476.3 1.3 collective-permute-start.27
  477.7 1.1 fusion.13
  478.8 1.3 collective-permute-done.27
  481.2 1.3 fusion.18
  482.5 3.6 collective-permute-done.9
  486.1 1.1 fusion.15
  488.2 5.8 %all-to-all-start.4 = ((bf16[8,28,1024]{2,1,0:T(8,128)(2,1)}), bf16[8,28,1024]{2,1,0:T(8,128)(2,1)S(1)}, u32[]{:S(2)}, u32[]{:S(2)}) async-start(bf16[8,28,1024]{2,1,0:T(8,128)(2,1)} %reshape.94), calls=%async_computation.4 | async-start | bytes 1048576 | tf_op jit(solution)/shard_map/all_to_all | solution.py:510
  494.0 2.8 copy-done.1
  496.8 7.4 %return_input.1 = f32[256,1024]{1,0:T(8,128)} custom-call(f32[256,1024]{1,0:T(8,128)S(1)} %copy-done.2, bf16[8,3,256,128]{3,2,1,0:T(8,128)(2,1)S(1)} %all_to_all.27.grad_ref.own_ref, bf16[1024,3072]{1,0:T(8,128)(2,1)S(1)} %copy-done.1), custom_call_target="tpu_custom_call" | custom-call | flops 1610612736 | bytes 8388608 | tf_op jit(solution)/shard_map/return_input/pallas_call | solution.py:487
  504.2 1.1 all-to-all-done.4
  505.4 37.4 %all-gather = bf16[8,28,1024]{2,1,0:T(8,128)(2,1)S(1)} all-gather(bf16[1,28,1024]{2,1,0:T(8,128)(2,1)S(1)} %bitcast.130), channel_id=1, replica_groups=mesh['z'=4,'yh'=2,'x'=4,'yl'=2,'core'=2] {'z','yh'}, dimensions={0}, use_global_device_ids=true | all-gather | bytes 516096 | tf_op jit(solution)/shard_map/all_gather | solution.py:572
  544.4 2.6 reshape.114
  547.1 1.3 fusion.19
  548.4 1.3 fusion.20
  549.7 1.0 fusion.21
  550.7 1.4 slice_bitcast_fusion.24
  552.1 1.3 slice.307
  553.3 1.1 pad_maximum_fusion.2
  555.1 1.0 pad_maximum_fusion.1
  (127 shorter events, 18.7 us)
Async XLA Ops:
  7.2 2.9 copy-start.10
  7.2 2.9 copy-start.11
  7.2 2.9 copy-start.12
  7.2 2.9 copy-start.13
  7.2 2.9 copy-start.14
  7.2 2.9 copy-start.18
  7.2 2.9 copy-start.15
  7.3 2.9 copy-start.16
  7.3 2.9 copy-start.17
  7.3 47.1 %copy-start.3 = (bf16[1,256,1024]{2,1,0:T(8,128)(2,1)S(1)}, bf16[1,256,1024]{2,1,0:T(8,128)(2,1)}, u32[]{:S(2)}) copy-start(bf16[1,256,1024]{2,1,0:T(8,128)(2,1)} %param.15) | copy-start | bytes 1572868
  7.3 47.1 %all-gather.8.cloned.1.call-start = ((), (), s32[]{:S(2)}) async-start(), calls=%async_computation.5 | async-start | bytes 6684672 | tf_op jit(solution)/shard_map/all_gather | solution.py:506
  8.0 111.7 %all-gather.10.cloned.1.call-start = ((), (), s32[]{:S(2)}) async-start(), calls=%async_computation.6 | async-start | bytes 2228224 | tf_op jit(solution)/shard_map/all_gather | solution.py:506
  8.8 143.5 %all-gather.12.cloned.1.call-start = ((), (), s32[]{:S(2)}) async-start(), calls=%async_computation.7 | async-start | bytes 8912896 | tf_op jit(solution)/shard_map/all_gather | solution.py:506
  9.5 197.0 %all-gather.14.cloned.1.call-start = ((), (), s32[]{:S(2)}) async-start(), calls=%async_computation.8 | async-start | bytes 8912896 | tf_op jit(solution)/shard_map/all_gather | solution.py:506
  54.4 2.8 copy-start
  113.9 1.0 copy-start.5
  114.8 21.5 %all-to-all-start.1 = ((bf16[8,256,128]{2,1,0:T(8,128)(2,1)}), bf16[8,256,128]{2,1,0:T(8,128)(2,1)S(1)}, u32[]{:S(2)}, u32[]{:S(2)}) async-start(bf16[8,256,128]{2,1,0:T(8,128)(2,1)} %get-tuple-element.34), calls=%async_computation.1 | async-start | bytes 1048576 | tf_op jit(solution)/shard_map/all_to_all | solution.py:510
  118.3 426.1 %all-gather.16.cloned.1.call-start = ((), (), s32[]{:S(2)}) async-start(), calls=%async_computation.9 | async-start | bytes 1474560 | tf_op jit(solution)/shard_map/all_gather | solution.py:568
  136.4 70.2 %copy-start.9 = (bf16[8,256,128]{2,1,0:T(8,128)(2,1)}, bf16[8,256,128]{2,1,0:T(8,128)(2,1)S(1)}, u32[]{:S(2)}) copy-start(bf16[8,256,128]{2,1,0:T(8,128)(2,1)S(1)} %all-to-all-done.1.att_ref) | copy-start | bytes 1572868
  206.5 42.6 %copy-start.6 = (f32[8,256,128]{2,1,0:T(8,128)S(1)}, f32[8,256,128]{2,1,0:T(8,128)}, u32[]{:S(2)}) copy-start(f32[8,256,128]{2,1,0:T(8,128)} %copy-done.5) | copy-start | bytes 3145732
  230.0 105.1 %collective-permute-start.10 = (bf16[272,12288]{1,0:T(8,128)(2,1)}, bf16[272,12288]{1,0:T(8,128)(2,1)}, u32[]{:S(2)}, u32[]{:S(2)}) collective-permute-start(bf16[272,12288]{1,0:T(8,128)(2,1)} %get-tuple-element.44.own_ref), channel_id=1, source_target_pairs={{0,1},{1,0},{4,5},{5,4},{8,9},{9,8},{12,13},{13,12},{2,3},{3,2},{6... | collective-permute-start | bytes 20054024 | tf_op jit(solution)/shard_map/ppermute | solution.py:46
  272.9 25.4 %copy-start.4 = (bf16[1,256,1024]{2,1,0:T(8,128)(2,1)S(1)}, bf16[1,256,1024]{2,1,0:T(8,128)(2,1)}, u32[]{:S(2)}) copy-start(bf16[1,256,1024]{2,1,0:T(8,128)(2,1)} %param.15) | copy-start | bytes 1572868
  298.3 4.3 collective-permute-start.1
  298.3 3.8 collective-permute-start
  302.6 4.7 copy-start.19
  306.8 23.9 %collective-permute-start.2 = (bf16[4,112,1024]{2,1,0:T(8,128)(2,1)}, bf16[4,112,1024]{2,1,0:T(8,128)(2,1)}, u32[]{:S(2)}, u32[]{:S(2)}) collective-permute-start(bf16[4,112,1024]{2,1,0:T(8,128)(2,1)} %get-tuple-element.41), channel_id=1, source_target_pairs={{0,2},{1,3},{4,6},{5,7},{8,10},{9,11},{12,14},{13,15},{2,16},{3,17... | collective-permute-start | bytes 2752520 | tf_op jit(solution)/shard_map/ppermute | solution.py:46
  308.6 33.4 %collective-permute-start.6 = (bf16[4,112,1024]{2,1,0:T(8,128)(2,1)S(1)}, bf16[4,112,1024]{2,1,0:T(8,128)(2,1)S(1)}, u32[]{:S(2)}, u32[]{:S(2)}) collective-permute-start(bf16[4,112,1024]{2,1,0:T(8,128)(2,1)S(1)} %get-tuple-element.43), channel_id=1, source_target_pairs={{0,18},{1,19},{4,22},{5,23},{8,26},{9,27},{12,30},{13,31},{2,0},{3... | collective-permute-start | bytes 2752520 | tf_op jit(solution)/shard_map/ppermute | solution.py:46
  332.3 13.6 %copy-start.7 = (bf16[4,112,1024]{2,1,0:T(8,128)(2,1)}, bf16[4,112,1024]{2,1,0:T(8,128)(2,1)S(1)}, u32[]{:S(2)}) copy-start(bf16[4,112,1024]{2,1,0:T(8,128)(2,1)S(1)} %add_convert_fusion.5) | copy-start | bytes 2752516
  333.1 12.8 %collective-permute-start.3 = (bf16[112,1024]{1,0:T(8,128)(2,1)S(1)}, bf16[112,1024]{1,0:T(8,128)(2,1)S(1)}, u32[]{:S(2)}, u32[]{:S(2)}) collective-permute-start(bf16[112,1024]{1,0:T(8,128)(2,1)S(1)} %get-tuple-element.81), channel_id=1, source_target_pairs={{0,4},{1,5},{4,8},{5,9},{8,12},{9,13},{12,0},{13,1},{2,6},{3,7},{6... | collective-permute-start | bytes 688136 | tf_op jit(solution)/shard_map/ppermute | solution.py:46
  333.9 147.3 %collective-permute-start.5 = (bf16[112,1024]{1,0:T(8,128)(2,1)}, bf16[112,1024]{1,0:T(8,128)(2,1)}, u32[]{:S(2)}, u32[]{:S(2)}) collective-permute-start(bf16[112,1024]{1,0:T(8,128)(2,1)} %get-tuple-element.82), channel_id=1, source_target_pairs={{0,12},{1,13},{4,0},{5,1},{8,4},{9,5},{12,8},{13,9},{2,14},{3,15},... | collective-permute-start | bytes 688136 | tf_op jit(solution)/shard_map/ppermute | solution.py:46
  341.9 30.3 %collective-permute-start.19 = (bf16[4,144,1024]{2,1,0:T(8,128)(2,1)S(1)}, bf16[4,144,1024]{2,1,0:T(8,128)(2,1)}, u32[]{:S(2)}, u32[]{:S(2)}) collective-permute-start(bf16[4,144,1024]{2,1,0:T(8,128)(2,1)S(1)} %get-tuple-element.50), channel_id=1, source_target_pairs={{0,2},{1,3},{4,6},{5,7},{8,10},{9,11},{12,14},{13,15},{2,16},{3,17... | collective-permute-start | bytes 3538952 | tf_op jit(solution)/shard_map/ppermute | solution.py:46
  342.3 10.8 %copy-start.8 = (bf16[4,112,1024]{2,1,0:T(8,128)(2,1)}, bf16[4,112,1024]{2,1,0:T(8,128)(2,1)S(1)}, u32[]{:S(2)}) copy-start(bf16[4,112,1024]{2,1,0:T(8,128)(2,1)S(1)} %add_convert_fusion.4) | copy-start | bytes 2752516
  342.4 33.6 %collective-permute-start.23 = (bf16[4,144,1024]{2,1,0:T(8,128)(2,1)S(1)}, bf16[4,144,1024]{2,1,0:T(8,128)(2,1)}, u32[]{:S(2)}, u32[]{:S(2)}) collective-permute-start(bf16[4,144,1024]{2,1,0:T(8,128)(2,1)S(1)} %get-tuple-element.52), channel_id=1, source_target_pairs={{0,18},{1,19},{4,22},{5,23},{8,26},{9,27},{12,30},{13,31},{2,0},{3... | collective-permute-start | bytes 3538952 | tf_op jit(solution)/shard_map/ppermute | solution.py:46
  353.1 44.7 %collective-permute-start.11 = (bf16[4,160,1024]{2,1,0:T(8,128)(2,1)S(1)}, bf16[4,160,1024]{2,1,0:T(8,128)(2,1)S(1)}, u32[]{:S(2)}, u32[]{:S(2)}) collective-permute-start(bf16[4,160,1024]{2,1,0:T(8,128)(2,1)S(1)} %get-tuple-element.46), channel_id=1, source_target_pairs={{0,2},{1,3},{4,6},{5,7},{8,10},{9,11},{12,14},{13,15},{2,16},{3,17... | collective-permute-start | bytes 3932168 | tf_op jit(solution)/shard_map/ppermute | solution.py:46
  353.2 46.0 %collective-permute-start.15 = (bf16[4,160,1024]{2,1,0:T(8,128)(2,1)S(1)}, bf16[4,160,1024]{2,1,0:T(8,128)(2,1)S(1)}, u32[]{:S(2)}, u32[]{:S(2)}) collective-permute-start(bf16[4,160,1024]{2,1,0:T(8,128)(2,1)S(1)} %get-tuple-element.48), channel_id=1, source_target_pairs={{0,18},{1,19},{4,22},{5,23},{8,26},{9,27},{12,30},{13,31},{2,0},{3... | collective-permute-start | bytes 3932168 | tf_op jit(solution)/shard_map/ppermute | solution.py:46
  373.9 28.4 %collective-permute-start.20 = (bf16[144,1024]{1,0:T(8,128)(2,1)S(1)}, bf16[144,1024]{1,0:T(8,128)(2,1)S(1)}, u32[]{:S(2)}, u32[]{:S(2)}) collective-permute-start(bf16[144,1024]{1,0:T(8,128)(2,1)S(1)} %get-tuple-element.71), channel_id=1, source_target_pairs={{0,4},{1,5},{4,8},{5,9},{8,12},{9,13},{12,0},{13,1},{2,6},{3,7},{6... | collective-permute-start | bytes 884744 | tf_op jit(solution)/shard_map/ppermute | solution.py:46
  376.0 40.7 %collective-permute-start.22 = (bf16[144,1024]{1,0:T(8,128)(2,1)S(1)}, bf16[144,1024]{1,0:T(8,128)(2,1)S(1)}, u32[]{:S(2)}, u32[]{:S(2)}) collective-permute-start(bf16[144,1024]{1,0:T(8,128)(2,1)S(1)} %get-tuple-element.72), channel_id=1, source_target_pairs={{0,12},{1,13},{4,0},{5,1},{8,4},{9,5},{12,8},{13,9},{2,14},{3,15},... | collective-permute-start | bytes 884744 | tf_op jit(solution)/shard_map/ppermute | solution.py:46
  397.8 7.9 %collective-permute-start.25 = (bf16[144,1024]{1,0:T(8,128)(2,1)S(1)}, bf16[144,1024]{1,0:T(8,128)(2,1)S(1)}, u32[]{:S(2)}, u32[]{:S(2)}) collective-permute-start(bf16[144,1024]{1,0:T(8,128)(2,1)S(1)} %get-tuple-element.74), channel_id=1, source_target_pairs={{0,12},{1,13},{4,0},{5,1},{8,4},{9,5},{12,8},{13,9},{2,14},{3,15},... | collective-permute-start | bytes 884744 | tf_op jit(solution)/shard_map/ppermute | solution.py:46
  399.2 25.9 %collective-permute-start.24 = (bf16[144,1024]{1,0:T(8,128)(2,1)S(1)}, bf16[144,1024]{1,0:T(8,128)(2,1)S(1)}, u32[]{:S(2)}, u32[]{:S(2)}) collective-permute-start(bf16[144,1024]{1,0:T(8,128)(2,1)S(1)} %get-tuple-element.73), channel_id=1, source_target_pairs={{0,4},{1,5},{4,8},{5,9},{8,12},{9,13},{12,0},{13,1},{2,6},{3,7},{6... | collective-permute-start | bytes 884744 | tf_op jit(solution)/shard_map/ppermute | solution.py:46
  402.3 11.2 %collective-permute-start.12 = (bf16[160,1024]{1,0:T(8,128)(2,1)S(1)}, bf16[160,1024]{1,0:T(8,128)(2,1)S(1)}, u32[]{:S(2)}, u32[]{:S(2)}) collective-permute-start(bf16[160,1024]{1,0:T(8,128)(2,1)S(1)} %get-tuple-element.67), channel_id=1, source_target_pairs={{0,4},{1,5},{4,8},{5,9},{8,12},{9,13},{12,0},{13,1},{2,6},{3,7},{6... | collective-permute-start | bytes 983048 | tf_op jit(solution)/shard_map/ppermute | solution.py:46
  405.8 10.7 %collective-permute-start.17 = (bf16[160,1024]{1,0:T(8,128)(2,1)S(1)}, bf16[160,1024]{1,0:T(8,128)(2,1)S(1)}, u32[]{:S(2)}, u32[]{:S(2)}) collective-permute-start(bf16[160,1024]{1,0:T(8,128)(2,1)S(1)} %get-tuple-element.70), channel_id=1, source_target_pairs={{0,12},{1,13},{4,0},{5,1},{8,4},{9,5},{12,8},{13,9},{2,14},{3,15},... | collective-permute-start | bytes 983048 | tf_op jit(solution)/shard_map/ppermute | solution.py:46
  413.5 7.7 %collective-permute-start.21 = (bf16[144,1024]{1,0:T(8,128)(2,1)S(1)}, bf16[144,1024]{1,0:T(8,128)(2,1)S(1)}, u32[]{:S(2)}, u32[]{:S(2)}) collective-permute-start(bf16[144,1024]{1,0:T(8,128)(2,1)S(1)} %fusion.10), channel_id=1, source_target_pairs={{0,4},{1,5},{4,8},{5,9},{8,12},{9,13},{12,0},{13,1},{2,6},{3,7},{6... | collective-permute-start | bytes 884744 | tf_op jit(solution)/shard_map/ppermute | solution.py:46
  416.5 11.2 %collective-permute-start.26 = (bf16[144,1024]{1,0:T(8,128)(2,1)S(1)}, bf16[144,1024]{1,0:T(8,128)(2,1)S(1)}, u32[]{:S(2)}, u32[]{:S(2)}) collective-permute-start(bf16[144,1024]{1,0:T(8,128)(2,1)S(1)} %fusion.7), channel_id=1, source_target_pairs={{0,12},{1,13},{4,0},{5,1},{8,4},{9,5},{12,8},{13,9},{2,14},{3,15},... | collective-permute-start | bytes 884744 | tf_op jit(solution)/shard_map/ppermute | solution.py:46
  416.7 18.0 %collective-permute-start.14 = (bf16[160,1024]{1,0:T(8,128)(2,1)S(1)}, bf16[160,1024]{1,0:T(8,128)(2,1)S(1)}, u32[]{:S(2)}, u32[]{:S(2)}) collective-permute-start(bf16[160,1024]{1,0:T(8,128)(2,1)S(1)} %get-tuple-element.68), channel_id=1, source_target_pairs={{0,12},{1,13},{4,0},{5,1},{8,4},{9,5},{12,8},{13,9},{2,14},{3,15},... | collective-permute-start | bytes 983048 | tf_op jit(solution)/shard_map/ppermute | solution.py:46
  421.2 13.5 %collective-permute-start.13 = (bf16[160,1024]{1,0:T(8,128)(2,1)S(1)}, bf16[160,1024]{1,0:T(8,128)(2,1)S(1)}, u32[]{:S(2)}, u32[]{:S(2)}) collective-permute-start(bf16[160,1024]{1,0:T(8,128)(2,1)S(1)} %fusion.4), channel_id=1, source_target_pairs={{0,4},{1,5},{4,8},{5,9},{8,12},{9,13},{12,0},{13,1},{2,6},{3,7},{6... | collective-permute-start | bytes 983048 | tf_op jit(solution)/shard_map/ppermute | solution.py:46
  425.1 14.4 %collective-permute-start.16 = (bf16[160,1024]{1,0:T(8,128)(2,1)S(1)}, bf16[160,1024]{1,0:T(8,128)(2,1)S(1)}, u32[]{:S(2)}, u32[]{:S(2)}) collective-permute-start(bf16[160,1024]{1,0:T(8,128)(2,1)S(1)} %get-tuple-element.69), channel_id=1, source_target_pairs={{0,4},{1,5},{4,8},{5,9},{8,12},{9,13},{12,0},{13,1},{2,6},{3,7},{6... | collective-permute-start | bytes 983048 | tf_op jit(solution)/shard_map/ppermute | solution.py:46
  427.7 15.6 %collective-permute-start.18 = (bf16[160,1024]{1,0:T(8,128)(2,1)S(1)}, bf16[160,1024]{1,0:T(8,128)(2,1)S(1)}, u32[]{:S(2)}, u32[]{:S(2)}) collective-permute-start(bf16[160,1024]{1,0:T(8,128)(2,1)S(1)} %fusion.1), channel_id=1, source_target_pairs={{0,12},{1,13},{4,0},{5,1},{8,4},{9,5},{12,8},{13,9},{2,14},{3,15},... | collective-permute-start | bytes 983048 | tf_op jit(solution)/shard_map/ppermute | solution.py:46
  434.7 42.9 %collective-permute-start.8 = (bf16[112,1024]{1,0:T(8,128)(2,1)S(1)}, bf16[112,1024]{1,0:T(8,128)(2,1)}, u32[]{:S(2)}, u32[]{:S(2)}) collective-permute-start(bf16[112,1024]{1,0:T(8,128)(2,1)S(1)} %get-tuple-element.84), channel_id=1, source_target_pairs={{0,12},{1,13},{4,0},{5,1},{8,4},{9,5},{12,8},{13,9},{2,14},{3,15},... | collective-permute-start | bytes 688136 | tf_op jit(solution)/shard_map/ppermute | solution.py:46
  434.7 47.7 %collective-permute-start.7 = (bf16[112,1024]{1,0:T(8,128)(2,1)S(1)}, bf16[112,1024]{1,0:T(8,128)(2,1)}, u32[]{:S(2)}, u32[]{:S(2)}) collective-permute-start(bf16[112,1024]{1,0:T(8,128)(2,1)S(1)} %get-tuple-element.83), channel_id=1, source_target_pairs={{0,4},{1,5},{4,8},{5,9},{8,12},{9,13},{12,0},{13,1},{2,6},{3,7},{6... | collective-permute-start | bytes 688136 | tf_op jit(solution)/shard_map/ppermute | solution.py:46
  439.6 41.6 %collective-permute-start.4 = (bf16[112,1024]{1,0:T(8,128)(2,1)}, bf16[112,1024]{1,0:T(8,128)(2,1)}, u32[]{:S(2)}, u32[]{:S(2)}) collective-permute-start(bf16[112,1024]{1,0:T(8,128)(2,1)} %fusion.16), channel_id=1, source_target_pairs={{0,4},{1,5},{4,8},{5,9},{8,12},{9,13},{12,0},{13,1},{2,6},{3,7},{6... | collective-permute-start | bytes 688136 | tf_op jit(solution)/shard_map/ppermute | solution.py:46
  476.3 3.8 collective-permute-start.27
  478.8 7.3 %collective-permute-start.9 = (bf16[112,1024]{1,0:T(8,128)(2,1)S(1)}, bf16[112,1024]{1,0:T(8,128)(2,1)S(1)}, u32[]{:S(2)}, u32[]{:S(2)}) collective-permute-start(bf16[112,1024]{1,0:T(8,128)(2,1)S(1)} %fusion.13), channel_id=1, source_target_pairs={{0,12},{1,13},{4,0},{5,1},{8,4},{9,5},{12,8},{13,9},{2,14},{3,15},... | collective-permute-start | bytes 688136 | tf_op jit(solution)/shard_map/ppermute | solution.py:46
  487.2 6.7 %copy-start.2 = (f32[256,1024]{1,0:T(8,128)S(1)}, f32[256,1024]{1,0:T(8,128)}, u32[]{:S(2)}) copy-start(f32[256,1024]{1,0:T(8,128)} %get-tuple-element.36.dmixed_ref) | copy-start | bytes 3145732
  488.2 17.1 %all-to-all-start.4 = ((bf16[8,28,1024]{2,1,0:T(8,128)(2,1)}), bf16[8,28,1024]{2,1,0:T(8,128)(2,1)S(1)}, u32[]{:S(2)}, u32[]{:S(2)}) async-start(bf16[8,28,1024]{2,1,0:T(8,128)(2,1)} %reshape.94), calls=%async_computation.4 | async-start | bytes 1048576 | tf_op jit(solution)/shard_map/all_to_all | solution.py:510
  494.0 2.8 copy-start.1
Sparse Core Ops, SparseCore 0:
  9.8 44.4 all-gather.7
  56.1 36.0 all-gather.9
  93.8 58.3 all-gather.11
  153.8 52.6 all-gather.13
  481.3 51.2 all-gather.15
